TPU v7x, 32 devices: a whole 2x2x4 slice. The times are simulated.
32 devices in a mesh: seq: 16 (over z, y, x), head: 2 (over core).
Axes of the slice: x: 2, y: 2, z: 4, core: 2. Of those that a mesh axis runs over, the one named last changes fastest.
Arguments:
- value_rows: bfloat16 [4096, 4096], P('seq', 'head'), may hold values from -6 to 6
- key_rows: bfloat16 [4096, 4096], P('seq', 'head'), may hold values from -6 to 6
- query_rows: bfloat16 [4096, 4096], P('seq', 'head'), may hold values from -6 to 6
- cotangent: bfloat16 [4096, 4096], P('seq', 'head'), may hold values from -6 to 6
- filter_taps: float32 [16, 2048], replicated, may hold values from -0.125 to 0.125
- doc_blocks: int32 [32], replicated, may hold values from 0 to 7, never falling along the last dimension, each value on 1 to 12 neighbouring positions
Outputs:
- output_rows: bfloat16 [4096, 4096], P('seq', 'head')
- grad_query: bfloat16 [4096, 4096], P('seq', 'head')
- grad_key: bfloat16 [4096, 4096], P('seq', 'head')
- grad_value: bfloat16 [4096, 4096], P('seq', 'head')
- grad_filter: float32 [16, 2048], replicated
Inputs may be any that keep to these rules, and one draw needn't show every extreme that they name: doc_blocks gives each 128-token block its document number; numbers never fall, each document spans 1 to 12 blocks, and one spans exactly 12.
All inputs are finite; a program needn't handle non-finite values.
Results may differ from a plain program's by a relative error of at most 0.0058.
Values may be sent and summed in bfloat16 or wider, within the bound.
A program may use at most 384 MiB of HBM per device.

v0:
```python
import jax
import jax.numpy as jnp
from jax import lax
from jax.sharding import PartitionSpec as P

DH = 64
BLK = 128


def passed_along(value, axis, by):
    length = lax.axis_size(axis)
    pairs = [(i, i + by) for i in range(length) if 0 <= i + by < length]
    return lax.ppermute(value, axis, pairs)


def toeplitz_blocks(filter_taps, block_len, lags_count):
    filters, taps_total = filter_taps.shape
    rounded = filter_taps.astype(jnp.bfloat16)
    padded = jnp.concatenate(
        [
            jnp.zeros((filters, block_len), jnp.bfloat16),
            rounded,
            jnp.zeros((filters, 2 * block_len), jnp.bfloat16),
        ],
        1,
    )
    rows_all = padded[:, 1 : 1 + (lags_count + 1) * block_len].reshape(
        filters, lags_count + 1, block_len
    )
    windows = jnp.concatenate([rows_all[:, :lags_count], rows_all[:, 1:]], 2)
    flipped = windows[..., ::-1]
    shifted = jnp.concatenate(
        [flipped[..., 1:], jnp.zeros((filters, lags_count, 1), jnp.bfloat16)], 2
    )
    repeated = jnp.broadcast_to(
        shifted[:, :, None, :], (filters, lags_count, block_len, 2 * block_len)
    )
    flat = repeated.reshape(filters, lags_count, 2 * block_len * block_len)
    sheared = flat[..., block_len - 1 : block_len - 1 + block_len * (2 * block_len - 1)]
    sheared = sheared.reshape(filters, lags_count, block_len, 2 * block_len - 1)
    return sheared[..., :block_len]


def diagonal_taps(grad_blocks, taps_total):
    filters, lags_count, block_len, _ = grad_blocks.shape
    flipped = grad_blocks[..., ::-1]
    padded = jnp.pad(flipped, ((0, 0), (0, 0), (0, 0), (0, block_len)))
    flat = padded.reshape(filters, lags_count, 2 * block_len * block_len)
    flat = flat[..., : block_len * (2 * block_len - 1)]
    sheared = flat.reshape(filters, lags_count, block_len, 2 * block_len - 1)
    diagonals = jnp.sum(sheared, axis=2)
    forward_part = diagonals[..., block_len - 1 :].reshape(filters, lags_count * block_len)
    backward_part = jnp.pad(diagonals[..., : block_len - 1], ((0, 0), (0, 0), (1, 0)))
    backward_part = backward_part.reshape(filters, lags_count * block_len)
    backward_part = jnp.concatenate(
        [backward_part[:, block_len:], jnp.zeros((filters, block_len), jnp.float32)], 1
    )
    return (forward_part + backward_part)[:, :taps_total]


def per_device(value_rows, key_rows, query_rows, cotangent, filter_taps, doc_blocks):
    tok_rows, channels = value_rows.shape
    filters, taps_total = filter_taps.shape
    block_len = BLK
    head_size = DH
    groups = channels // (filters * head_size)
    blocks_dev = tok_rows // block_len
    reach_count = taps_total // tok_rows
    lags_count = taps_total // block_len + 1
    margin = reach_count * blocks_dev
    toeplitz = toeplitz_blocks(filter_taps, block_len, lags_count)
    product = (key_rows.astype(jnp.float32) * value_rows.astype(jnp.float32)).astype(jnp.bfloat16)
    scaled = (cotangent.astype(jnp.float32) * query_rows.astype(jnp.float32)).astype(jnp.bfloat16)
    earlier_parts = []
    later_parts = []
    moving_back = product
    moving_fore = scaled
    for distance in range(reach_count):
        moving_back = passed_along(moving_back, "seq", 1)
        moving_fore = passed_along(moving_fore, "seq", -1)
        earlier_parts.append(moving_back)
        later_parts.append(moving_fore)
    with_past = jnp.concatenate(earlier_parts[::-1] + [product], 0)
    with_future = jnp.concatenate([scaled] + later_parts, 0)
    shape5 = (-1, block_len, groups, filters, head_size)
    past_blocks = with_past.reshape(shape5)
    future_blocks = with_future.reshape(shape5)
    own_scaled = scaled.reshape(shape5)
    shard_index = lax.axis_index("seq")
    padded = jnp.concatenate(
        [jnp.full((margin,), -1, jnp.int32), doc_blocks, jnp.full((margin,), -2, jnp.int32)], 0
    )
    window = lax.dynamic_slice_in_dim(padded, shard_index * blocks_dev, 2 * margin + blocks_dev)
    own_docs = window[margin : margin + blocks_dev]
    back_mask = jnp.stack(
        [window[margin - b : margin - b + blocks_dev] == own_docs for b in range(lags_count)], 1
    )
    fore_mask = jnp.stack(
        [window[margin + b : margin + b + blocks_dev] == own_docs for b in range(lags_count)], 1
    )
    back_weight = back_mask.astype(jnp.bfloat16)
    fore_weight = fore_mask.astype(jnp.bfloat16)
    stacked = jnp.stack(
        [past_blocks[margin - b : margin - b + blocks_dev] for b in range(lags_count)], 1
    )
    stacked = stacked * back_weight[:, :, None, None, None, None]
    convolved = jnp.einsum(
        "fbrs,nbsgfd->nrgfd", toeplitz, stacked, preferred_element_type=jnp.float32
    )
    grad_blocks = jnp.einsum(
        "nrgfd,nbsgfd->fbrs", own_scaled, stacked, preferred_element_type=jnp.float32
    )
    fore_stack = jnp.stack([future_blocks[b : b + blocks_dev] for b in range(lags_count)], 1)
    fore_stack = fore_stack * fore_weight[:, :, None, None, None, None]
    adjoint = jnp.einsum(
        "fbrs,nbrgfd->nsgfd", toeplitz, fore_stack, preferred_element_type=jnp.float32
    )
    taps_grad = diagonal_taps(grad_blocks, taps_total) * (1.0 / (tok_rows * lax.axis_size("seq")))
    grad_filter = lax.psum(taps_grad, ("seq", "head"))
    convolved = convolved.reshape(tok_rows, channels)
    adjoint = adjoint.reshape(tok_rows, channels)
    output_rows = (query_rows.astype(jnp.float32) * convolved).astype(jnp.bfloat16)
    grad_query = (cotangent.astype(jnp.float32) * convolved).astype(jnp.bfloat16)
    grad_key = (adjoint * value_rows.astype(jnp.float32)).astype(jnp.bfloat16)
    grad_value = (adjoint * key_rows.astype(jnp.float32)).astype(jnp.bfloat16)
    return (output_rows, grad_query, grad_key, grad_value, grad_filter)


def solution(mesh):
    in_specs = (P("seq", "head"), P("seq", "head"), P("seq", "head"), P("seq", "head"), P(), P())
    out_specs = (P("seq", "head"), P("seq", "head"), P("seq", "head"), P("seq", "head"), P())
    return jax.shard_map(
        per_device, mesh=mesh, in_specs=in_specs, out_specs=out_specs, check_vma=False
    )
```

profile of v0, /device:TPU:0, one launch (start us, length us, event | category | flops | bytes accessed | tf_op | source)
XLA Modules:
  0.0 1192.5 jit_solution(1083632972342527251)
XLA Ops:
  12.2 26.7 %collective-permute-done.8 = bf16[256,2048]{0,1:T(8,128)(2,1)S(1)} collective-permute-done((bf16[256,2048]{0,1:T(8,128)(2,1)S(1)}, bf16[256,2048]{0,1:T(8,128)(2,1)S(1)}, u32[]{:S(2)}, u32[]{:S(2)}) %collective-permute-start.8) | collective-permute-done | bytes 1048608 | tf_op jit(solution)/shard_map/ppermute | solution.py:13
  41.1 25.5 %collective-permute-done.9 = bf16[256,2048]{0,1:T(8,128)(2,1)S(1)} collective-permute-done((bf16[256,2048]{0,1:T(8,128)(2,1)S(1)}, bf16[256,2048]{0,1:T(8,128)(2,1)S(1)}, u32[]{:S(2)}, u32[]{:S(2)}) %collective-permute-start.9) | collective-permute-done | bytes 1048608 | tf_op jit(solution)/shard_map/ppermute | solution.py:13
  68.9 24.6 %collective-permute-done.10 = bf16[256,2048]{0,1:T(8,128)(2,1)S(1)} collective-permute-done((bf16[256,2048]{0,1:T(8,128)(2,1)S(1)}, bf16[256,2048]{0,1:T(8,128)(2,1)S(1)}, u32[]{:S(2)}, u32[]{:S(2)}) %collective-permute-start.10) | collective-permute-done | bytes 1048608 | tf_op jit(solution)/shard_map/ppermute | solution.py:13
  95.8 23.7 %collective-permute-done.11 = bf16[256,2048]{0,1:T(8,128)(2,1)S(1)} collective-permute-done((bf16[256,2048]{0,1:T(8,128)(2,1)S(1)}, bf16[256,2048]{0,1:T(8,128)(2,1)S(1)}, u32[]{:S(2)}, u32[]{:S(2)}) %collective-permute-start.11) | collective-permute-done | bytes 1048608 | tf_op jit(solution)/shard_map/ppermute | solution.py:13
  121.7 22.8 %collective-permute-done.12 = bf16[256,2048]{0,1:T(8,128)(2,1)S(1)} collective-permute-done((bf16[256,2048]{0,1:T(8,128)(2,1)S(1)}, bf16[256,2048]{0,1:T(8,128)(2,1)S(1)}, u32[]{:S(2)}, u32[]{:S(2)}) %collective-permute-start.12) | collective-permute-done | bytes 1048608 | tf_op jit(solution)/shard_map/ppermute | solution.py:13
  146.8 23.2 %collective-permute-done.13 = bf16[256,2048]{0,1:T(8,128)(2,1)} collective-permute-done((bf16[256,2048]{0,1:T(8,128)(2,1)S(1)}, bf16[256,2048]{0,1:T(8,128)(2,1)}, u32[]{:S(2)}, u32[]{:S(2)}) %collective-permute-start.13) | collective-permute-done | bytes 1048608 | tf_op jit(solution)/shard_map/ppermute | solution.py:13
  179.1 14.3 %collective-permute-done.14 = bf16[256,2048]{0,1:T(8,128)(2,1)} collective-permute-done((bf16[256,2048]{0,1:T(8,128)(2,1)}, bf16[256,2048]{0,1:T(8,128)(2,1)}, u32[]{:S(2)}, u32[]{:S(2)}) %collective-permute-start.14) | collective-permute-done | bytes 1048608 | tf_op jit(solution)/shard_map/ppermute | solution.py:13
  195.4 6.5 broadcast_in_dim.8
  201.9 27.2 %reshape.378 = bf16[16,17,32768]{2,0,1:T(8,128)(2,1)} reshape(bf16[16,17,128,256]{3,2,0,1:T(8,128)(2,1)} %broadcast_in_dim.8) | data formatting | bytes 35651584 | tf_op jit(solution)/shard_map/reshape | solution.py:38
  229.1 16.6 %slice.318 = bf16[16,17,32640]{2,0,1:T(8,128)(2,1)} slice(bf16[16,17,32768]{2,0,1:T(8,128)(2,1)} %reshape.378), slice={[0:16], [0:17], [127:32767]} | slice | bytes 35512320 | tf_op jit(solution)/shard_map/slice | solution.py:39
  245.7 60.3 %reshape.379 = bf16[16,17,128,255]{3,2,0,1:T(8,128)(2,1)} reshape(bf16[16,17,32640]{2,0,1:T(8,128)(2,1)} %slice.318) | data formatting | bytes 35512320 | tf_op jit(solution)/shard_map/reshape | solution.py:40
  324.7 5.1 pad_maximum_fusion
  347.6 3.6 constant_dynamic-update-slice_fusion.32
  354.6 3.5 constant_dynamic-update-slice_fusion.30
  368.5 3.5 constant_dynamic-update-slice_fusion.26
  393.6 20.3 %broadcast_multiply_fusion = bf16[2,17,128,2,16,64]{2,0,5,4,3,1:T(2,128)(2,1)} fusion(bf16[2,17,128,2,16,64]{2,0,5,4,3,1:T(2,128)(2,1)} %constant_dynamic-update-slice_fusion.17, bf16[2,17]{0,1:T(8,128)(2,1)S(1)} %copy.106), kind=kLoop, calls=%fused_computation.7 | loop fusion | flops 8912896 | bytes 35651652 | tf_op jit(solution)/shard_map/mul | solution.py:114
  413.9 11.4 fusion.18
  428.9 5.6 collective-permute-start
  434.4 18.7 %collective-permute-done = bf16[256,2048]{0,1:T(8,128)(2,1)S(1)} collective-permute-done((bf16[256,2048]{0,1:T(8,128)(2,1)S(1)}, bf16[256,2048]{0,1:T(8,128)(2,1)S(1)}, u32[]{:S(2)}, u32[]{:S(2)}) %collective-permute-start) | collective-permute-done | bytes 1048608 | tf_op jit(solution)/shard_map/ppermute | solution.py:13
  453.1 4.5 collective-permute-start.1
  457.6 18.9 %collective-permute-done.1 = bf16[256,2048]{0,1:T(8,128)(2,1)S(1)} collective-permute-done((bf16[256,2048]{0,1:T(8,128)(2,1)S(1)}, bf16[256,2048]{0,1:T(8,128)(2,1)S(1)}, u32[]{:S(2)}, u32[]{:S(2)}) %collective-permute-start.1) | collective-permute-done | bytes 1048608 | tf_op jit(solution)/shard_map/ppermute | solution.py:13
  476.5 4.4 collective-permute-start.2
  480.9 18.9 %collective-permute-done.2 = bf16[256,2048]{0,1:T(8,128)(2,1)S(1)} collective-permute-done((bf16[256,2048]{0,1:T(8,128)(2,1)S(1)}, bf16[256,2048]{0,1:T(8,128)(2,1)S(1)}, u32[]{:S(2)}, u32[]{:S(2)}) %collective-permute-start.2) | collective-permute-done | bytes 1048608 | tf_op jit(solution)/shard_map/ppermute | solution.py:13
  499.8 4.4 collective-permute-start.3
  504.3 18.9 %collective-permute-done.3 = bf16[256,2048]{0,1:T(8,128)(2,1)S(1)} collective-permute-done((bf16[256,2048]{0,1:T(8,128)(2,1)S(1)}, bf16[256,2048]{0,1:T(8,128)(2,1)S(1)}, u32[]{:S(2)}, u32[]{:S(2)}) %collective-permute-start.3) | collective-permute-done | bytes 1048608 | tf_op jit(solution)/shard_map/ppermute | solution.py:13
  523.2 4.4 collective-permute-start.4
  527.6 18.9 %collective-permute-done.4 = bf16[256,2048]{0,1:T(8,128)(2,1)S(1)} collective-permute-done((bf16[256,2048]{0,1:T(8,128)(2,1)S(1)}, bf16[256,2048]{0,1:T(8,128)(2,1)S(1)}, u32[]{:S(2)}, u32[]{:S(2)}) %collective-permute-start.4) | collective-permute-done | bytes 1048608 | tf_op jit(solution)/shard_map/ppermute | solution.py:13
  546.5 4.4 collective-permute-start.5
  550.9 18.4 %collective-permute-done.5 = bf16[256,2048]{0,1:T(8,128)(2,1)S(1)} collective-permute-done((bf16[256,2048]{0,1:T(8,128)(2,1)S(1)}, bf16[256,2048]{0,1:T(8,128)(2,1)S(1)}, u32[]{:S(2)}, u32[]{:S(2)}) %collective-permute-start.5) | collective-permute-done | bytes 1048608 | tf_op jit(solution)/shard_map/ppermute | solution.py:13
  569.4 6.6 collective-permute-start.6
  576.0 18.2 %collective-permute-done.6 = bf16[256,2048]{0,1:T(8,128)(2,1)} collective-permute-done((bf16[256,2048]{0,1:T(8,128)(2,1)S(1)}, bf16[256,2048]{0,1:T(8,128)(2,1)}, u32[]{:S(2)}, u32[]{:S(2)}) %collective-permute-start.6) | collective-permute-done | bytes 1048608 | tf_op jit(solution)/shard_map/ppermute | solution.py:13
  594.1 5.5 collective-permute-start.7
  627.1 5.2 pad_maximum_fusion.8
  650.0 3.6 constant_dynamic-update-slice_fusion.15
  660.5 3.5 constant_dynamic-update-slice_fusion.12
  674.4 3.5 constant_dynamic-update-slice_fusion.8
  694.8 20.3 %broadcast_multiply_fusion.1 = bf16[2,17,128,2,16,64]{2,0,5,4,3,1:T(2,128)(2,1)} fusion(bf16[2,17,128,2,16,64]{2,0,5,4,3,1:T(2,128)(2,1)} %constant_dynamic-update-slice_fusion, bf16[2,17]{0,1:T(8,128)(2,1)S(1)} %copy.84), kind=kLoop, calls=%fused_computation.8 | loop fusion | flops 8912896 | bytes 35651652 | tf_op jit(solution)/shard_map/mul | solution.py:106
  715.1 12.6 %fusion.15 = f32[2,128,2,16,64]{1,4,2,0,3:T(8,128)} fusion(bf16[2,17,128,2,16,64]{2,0,5,4,3,1:T(2,128)(2,1)} %broadcast_multiply_fusion.1, bf16[16,17,128,255]{3,2,0,1:T(8,128)(2,1)} %reshape.379), kind=kOutput, calls=%fused_computation.22 | convolution fusion | flops 2281701376 | bytes 28835840 | tf_op jit(solution)/shard_map/fbrs,nbsgfd->nrgfd/dot_general | solution.py:107
  727.7 13.0 %fusion.6 = f32[16,17,128,128]{2,3,1,0:T(8,128)} fusion(bf16[2,17,128,2,16,64]{2,0,5,4,3,1:T(2,128)(2,1)} %broadcast_multiply_fusion.1, bf16[2,128,2,16,64,1]{1,0,4,3,2,5:T(2,128)(2,1)S(1)} %bitcast.199), kind=kOutput, calls=%fused_computation.9 | convolution fusion | flops 2281701376 | bytes 36700160 | tf_op jit(solution)/shard_map/nrgfd,nbsgfd->fbrs/dot_general | solution.py:110
  740.7 133.7 %rev.4 = f32[16,17,128,128]{2,3,1,0:T(8,128)} reverse(f32[16,17,128,128]{2,3,1,0:T(8,128)} %fusion.6), dimensions={3} | reverse | bytes 35651584 | tf_op jit(solution)/shard_map/rev | solution.py:46
  874.4 18.3 %copy.127 = f32[16,17,128,128]{3,2,0,1:T(8,128)} copy(f32[16,17,128,128]{2,3,1,0:T(8,128)} %rev.4) | data formatting | bytes 35651584
  892.7 19.7 %pad.10.clone = f32[16,17,128,256]{3,2,0,1:T(8,128)} pad(f32[16,17,128,128]{3,2,0,1:T(8,128)} %copy.127, f32[]{:T(128)} %constant.26.clone.1), padding=0_0x0_0x0_0x0_128 | pad | bytes 53477380 | tf_op jit(solution)/shard_map/jit(_pad)/pad | solution.py:47
  912.3 38.1 %reshape.383 = f32[16,17,32768]{2,0,1:T(8,128)} reshape(f32[16,17,128,256]{3,2,0,1:T(8,128)} %pad.10.clone) | data formatting | bytes 71303168 | tf_op jit(solution)/shard_map/reshape | solution.py:48
  950.5 25.3 %slice.320 = f32[16,17,32640]{2,0,1:T(8,128)} slice(f32[16,17,32768]{2,0,1:T(8,128)} %reshape.383), slice={[0:16], [0:17], [0:32640]} | slice | bytes 71024640 | tf_op jit(solution)/shard_map/slice | solution.py:49
  975.7 58.3 %reshape.384 = f32[16,17,128,255]{3,2,0,1:T(8,128)} reshape(f32[16,17,32640]{2,0,1:T(8,128)} %slice.320) | data formatting | bytes 71024640 | tf_op jit(solution)/shard_map/reshape | solution.py:50
  1034.0 13.4 %reduce_sum.9 = f32[16,17,255]{2,0,1:T(8,128)S(1)} reduce(f32[16,17,128,255]{3,2,0,1:T(8,128)} %reshape.384, f32[]{:T(128)} %constant.26.clone.1), dimensions={2}, to_apply=%region_0.1 | reduce | flops 8808720 | bytes 35789764 | tf_op jit(solution)/shard_map/reduce_sum | solution.py:51
  1047.5 4.6 copy.88
  1059.7 124.0 %all-reduce.6.cloned.1.call-done = f32[16,2048]{1,0:T(8,128)} async-done(((f32[16,2048]{1,0:T(8,128)}), f32[16,2048]{1,0:T(8,128)}) %all-reduce.6.cloned.1.call-update) | async-done | bytes 131088 | tf_op jit(solution)/shard_map/psum | solution.py:119
  (224 shorter events, 191.0 us)
Async XLA Ops:
  7.2 1176.5 %all-reduce.6.cloned.1.call-start = ((), (), s32[]{:S(2)}) async-start(), calls=%async_computation | async-start | bytes 262144 | tf_op jit(solution)/shard_map/psum | solution.py:119
  8.7 220.4 %copy-start = (bf16[256,2048]{0,1:T(8,128)(2,1)}, bf16[256,2048]{0,1:T(8,128)(2,1)S(1)}, u32[]{:S(2)}) copy-start(bf16[256,2048]{0,1:T(8,128)(2,1)S(1)} %copy.89) | copy-start | bytes 3145732
  10.6 218.5 %copy-start.2 = (bf16[256,2048]{0,1:T(8,128)(2,1)}, bf16[256,2048]{0,1:T(8,128)(2,1)S(1)}, u32[]{:S(2)}) copy-start(bf16[256,2048]{0,1:T(8,128)(2,1)S(1)} %copy.65) | copy-start | bytes 3145732
  10.9 28.0 %collective-permute-start.8 = (bf16[256,2048]{0,1:T(8,128)(2,1)S(1)}, bf16[256,2048]{0,1:T(8,128)(2,1)S(1)}, u32[]{:S(2)}, u32[]{:S(2)}) collective-permute-start(bf16[256,2048]{0,1:T(8,128)(2,1)S(1)} %fusion.14), channel_id=1, source_target_pairs={{2,0},{4,2},{6,4},{8,6},{10,8},{12,10},{14,12},{16,14},{18,16},{20... | collective-permute-start | bytes 3145736 | tf_op jit(solution)/shard_map/ppermute | solution.py:13
  39.8 26.8 %collective-permute-start.9 = (bf16[256,2048]{0,1:T(8,128)(2,1)S(1)}, bf16[256,2048]{0,1:T(8,128)(2,1)S(1)}, u32[]{:S(2)}, u32[]{:S(2)}) collective-permute-start(bf16[256,2048]{0,1:T(8,128)(2,1)S(1)} %collective-permute-done.8), channel_id=1, source_target_pairs={{2,0},{4,2},{6,4},{8,6},{10,8},{12,10},{14,12},{16,14},{18,16},{20... | collective-permute-start | bytes 3145736 | tf_op jit(solution)/shard_map/ppermute | solution.py:13
  67.6 25.9 %collective-permute-start.10 = (bf16[256,2048]{0,1:T(8,128)(2,1)S(1)}, bf16[256,2048]{0,1:T(8,128)(2,1)S(1)}, u32[]{:S(2)}, u32[]{:S(2)}) collective-permute-start(bf16[256,2048]{0,1:T(8,128)(2,1)S(1)} %collective-permute-done.9), channel_id=1, source_target_pairs={{2,0},{4,2},{6,4},{8,6},{10,8},{12,10},{14,12},{16,14},{18,16},{20... | collective-permute-start | bytes 3145736 | tf_op jit(solution)/shard_map/ppermute | solution.py:13
  94.5 25.0 %collective-permute-start.11 = (bf16[256,2048]{0,1:T(8,128)(2,1)S(1)}, bf16[256,2048]{0,1:T(8,128)(2,1)S(1)}, u32[]{:S(2)}, u32[]{:S(2)}) collective-permute-start(bf16[256,2048]{0,1:T(8,128)(2,1)S(1)} %collective-permute-done.10), channel_id=1, source_target_pairs={{2,0},{4,2},{6,4},{8,6},{10,8},{12,10},{14,12},{16,14},{18,16},{20... | collective-permute-start | bytes 3145736 | tf_op jit(solution)/shard_map/ppermute | solution.py:13
  119.5 1.0 copy-start.10
  120.5 24.0 %collective-permute-start.12 = (bf16[256,2048]{0,1:T(8,128)(2,1)S(1)}, bf16[256,2048]{0,1:T(8,128)(2,1)S(1)}, u32[]{:S(2)}, u32[]{:S(2)}) collective-permute-start(bf16[256,2048]{0,1:T(8,128)(2,1)S(1)} %collective-permute-done.11), channel_id=1, source_target_pairs={{2,0},{4,2},{6,4},{8,6},{10,8},{12,10},{14,12},{16,14},{18,16},{20... | collective-permute-start | bytes 3145736 | tf_op jit(solution)/shard_map/ppermute | solution.py:13
  145.5 24.5 %collective-permute-start.13 = (bf16[256,2048]{0,1:T(8,128)(2,1)S(1)}, bf16[256,2048]{0,1:T(8,128)(2,1)}, u32[]{:S(2)}, u32[]{:S(2)}) collective-permute-start(bf16[256,2048]{0,1:T(8,128)(2,1)S(1)} %collective-permute-done.12), channel_id=1, source_target_pairs={{2,0},{4,2},{6,4},{8,6},{10,8},{12,10},{14,12},{16,14},{18,16},{20... | collective-permute-start | bytes 3145736 | tf_op jit(solution)/shard_map/ppermute | solution.py:13
  170.0 23.4 %collective-permute-start.14 = (bf16[256,2048]{0,1:T(8,128)(2,1)}, bf16[256,2048]{0,1:T(8,128)(2,1)}, u32[]{:S(2)}, u32[]{:S(2)}) collective-permute-start(bf16[256,2048]{0,1:T(8,128)(2,1)} %collective-permute-done.13), channel_id=1, source_target_pairs={{2,0},{4,2},{6,4},{8,6},{10,8},{12,10},{14,12},{16,14},{18,16},{20... | collective-permute-start | bytes 3145736 | tf_op jit(solution)/shard_map/ppermute | solution.py:13
  193.4 131.4 %collective-permute-start.15 = (bf16[256,2048]{0,1:T(8,128)(2,1)}, bf16[256,2048]{0,1:T(8,128)(2,1)}, u32[]{:S(2)}, u32[]{:S(2)}) collective-permute-start(bf16[256,2048]{0,1:T(8,128)(2,1)} %collective-permute-done.14), channel_id=1, source_target_pairs={{2,0},{4,2},{6,4},{8,6},{10,8},{12,10},{14,12},{16,14},{18,16},{20... | collective-permute-start | bytes 3145736 | tf_op jit(solution)/shard_map/ppermute | solution.py:13
  245.7 66.0 %copy-start.6 = (bf16[256,2048]{0,1:T(8,128)(2,1)S(1)}, bf16[256,2048]{0,1:T(8,128)(2,1)}, u32[]{:S(2)}) copy-start(bf16[256,2048]{0,1:T(8,128)(2,1)} %copy-done.5) | copy-start | bytes 3145732
  245.7 67.1 %copy-start.8 = (bf16[256,2048]{0,1:T(8,128)(2,1)S(1)}, bf16[256,2048]{0,1:T(8,128)(2,1)}, u32[]{:S(2)}) copy-start(bf16[256,2048]{0,1:T(8,128)(2,1)} %copy-done.7) | copy-start | bytes 3145732
  334.2 48.4 %copy-start.23 = (bf16[2,1,128,2,16,64]{2,0,5,4,3,1:T(2,128)(2,1)S(1)}, bf16[2,1,128,2,16,64]{2,0,5,4,3,1:T(2,128)(2,1)}, u32[]{:S(2)}) copy-start(bf16[2,1,128,2,16,64]{2,0,5,4,3,1:T(2,128)(2,1)} %stack.262) | copy-start | bytes 3145732
  338.6 47.7 %copy-start.21 = (bf16[2,1,128,2,16,64]{2,0,5,4,3,1:T(2,128)(2,1)S(1)}, bf16[2,1,128,2,16,64]{2,0,5,4,3,1:T(2,128)(2,1)}, u32[]{:S(2)}) copy-start(bf16[2,1,128,2,16,64]{2,0,5,4,3,1:T(2,128)(2,1)} %stack.264) | copy-start | bytes 3145732
  347.5 31.4 %copy-start.25 = (bf16[2,1,128,2,16,64]{2,0,5,4,3,1:T(2,128)(2,1)S(1)}, bf16[2,1,128,2,16,64]{2,0,5,4,3,1:T(2,128)(2,1)}, u32[]{:S(2)}) copy-start(bf16[2,1,128,2,16,64]{2,0,5,4,3,1:T(2,128)(2,1)} %stack.260) | copy-start | bytes 3145732
  347.5 33.2 %copy-start.30 = (bf16[2,1,128,2,16,64]{2,0,5,4,3,1:T(2,128)(2,1)S(1)}, bf16[2,1,128,2,16,64]{2,0,5,4,3,1:T(2,128)(2,1)}, u32[]{:S(2)}) copy-start(bf16[2,1,128,2,16,64]{2,0,5,4,3,1:T(2,128)(2,1)} %stack.261) | copy-start | bytes 3145732
  347.5 36.9 %copy-start.28 = (bf16[2,1,128,2,16,64]{2,0,5,4,3,1:T(2,128)(2,1)S(1)}, bf16[2,1,128,2,16,64]{2,0,5,4,3,1:T(2,128)(2,1)}, u32[]{:S(2)}) copy-start(bf16[2,1,128,2,16,64]{2,0,5,4,3,1:T(2,128)(2,1)} %stack.263) | copy-start | bytes 3145732
  347.5 40.6 %copy-start.26 = (bf16[2,1,128,2,16,64]{2,0,5,4,3,1:T(2,128)(2,1)S(1)}, bf16[2,1,128,2,16,64]{2,0,5,4,3,1:T(2,128)(2,1)}, u32[]{:S(2)}) copy-start(bf16[2,1,128,2,16,64]{2,0,5,4,3,1:T(2,128)(2,1)} %stack.265) | copy-start | bytes 3145732
  413.9 13.1 %copy-start.4 = (bf16[256,2048]{0,1:T(8,128)(2,1)S(1)}, bf16[256,2048]{0,1:T(8,128)(2,1)}, u32[]{:S(2)}) copy-start(bf16[256,2048]{0,1:T(8,128)(2,1)} %copy.66) | copy-start | bytes 3145732
  413.9 13.1 %copy-start.19 = (bf16[256,2048]{0,1:T(8,128)(2,1)S(1)}, bf16[256,2048]{0,1:T(8,128)(2,1)}, u32[]{:S(2)}) copy-start(bf16[256,2048]{0,1:T(8,128)(2,1)} %copy.67) | copy-start | bytes 3145732
  413.9 188.6 %copy-start.34 = (pred[2,1]{0,1:T(4,128)(4,1)S(1)}, pred[2,1]{0,1:T(4,128)(4,1)}, u32[]{:S(2)}) copy-start(pred[2,1]{0,1:T(4,128)(4,1)} %get-tuple-element.55) | copy-start | bytes 10
  413.9 188.7 %copy-start.33 = (pred[2,1]{0,1:T(4,128)(4,1)S(1)}, pred[2,1]{0,1:T(4,128)(4,1)}, u32[]{:S(2)}) copy-start(pred[2,1]{0,1:T(4,128)(4,1)} %get-tuple-element.54) | copy-start | bytes 10
  428.9 24.2 %collective-permute-start = (bf16[256,2048]{0,1:T(8,128)(2,1)S(1)}, bf16[256,2048]{0,1:T(8,128)(2,1)S(1)}, u32[]{:S(2)}, u32[]{:S(2)}) collective-permute-start(bf16[256,2048]{0,1:T(8,128)(2,1)S(1)} %get-tuple-element.17), channel_id=1, source_target_pairs={{0,2},{2,4},{4,6},{6,8},{8,10},{10,12},{12,14},{14,16},{16,18},{18... | collective-permute-start | bytes 3145736 | tf_op jit(solution)/shard_map/ppermute | solution.py:13
  453.1 122.9 %copy-start.12 = (bf16[256,2048]{0,1:T(8,128)(2,1)}, bf16[256,2048]{0,1:T(8,128)(2,1)S(1)}, u32[]{:S(2)}) copy-start(bf16[256,2048]{0,1:T(8,128)(2,1)S(1)} %collective-permute-done) | copy-start | bytes 3145732
  453.1 23.4 %collective-permute-start.1 = (bf16[256,2048]{0,1:T(8,128)(2,1)S(1)}, bf16[256,2048]{0,1:T(8,128)(2,1)S(1)}, u32[]{:S(2)}, u32[]{:S(2)}) collective-permute-start(bf16[256,2048]{0,1:T(8,128)(2,1)S(1)} %collective-permute-done), channel_id=1, source_target_pairs={{0,2},{2,4},{4,6},{6,8},{8,10},{10,12},{12,14},{14,16},{16,18},{18... | collective-permute-start | bytes 3145736 | tf_op jit(solution)/shard_map/ppermute | solution.py:13
  476.5 117.6 %copy-start.14 = (bf16[256,2048]{0,1:T(8,128)(2,1)}, bf16[256,2048]{0,1:T(8,128)(2,1)S(1)}, u32[]{:S(2)}) copy-start(bf16[256,2048]{0,1:T(8,128)(2,1)S(1)} %collective-permute-done.1) | copy-start | bytes 3145732
  476.5 23.3 %collective-permute-start.2 = (bf16[256,2048]{0,1:T(8,128)(2,1)S(1)}, bf16[256,2048]{0,1:T(8,128)(2,1)S(1)}, u32[]{:S(2)}, u32[]{:S(2)}) collective-permute-start(bf16[256,2048]{0,1:T(8,128)(2,1)S(1)} %collective-permute-done.1), channel_id=1, source_target_pairs={{0,2},{2,4},{4,6},{6,8},{8,10},{10,12},{12,14},{14,16},{16,18},{18... | collective-permute-start | bytes 3145736 | tf_op jit(solution)/shard_map/ppermute | solution.py:13
  499.8 94.3 %copy-start.15 = (bf16[256,2048]{0,1:T(8,128)(2,1)}, bf16[256,2048]{0,1:T(8,128)(2,1)S(1)}, u32[]{:S(2)}) copy-start(bf16[256,2048]{0,1:T(8,128)(2,1)S(1)} %collective-permute-done.2) | copy-start | bytes 3145732
  499.8 23.3 %collective-permute-start.3 = (bf16[256,2048]{0,1:T(8,128)(2,1)S(1)}, bf16[256,2048]{0,1:T(8,128)(2,1)S(1)}, u32[]{:S(2)}, u32[]{:S(2)}) collective-permute-start(bf16[256,2048]{0,1:T(8,128)(2,1)S(1)} %collective-permute-done.2), channel_id=1, source_target_pairs={{0,2},{2,4},{4,6},{6,8},{8,10},{10,12},{12,14},{14,16},{16,18},{18... | collective-permute-start | bytes 3145736 | tf_op jit(solution)/shard_map/ppermute | solution.py:13
  523.1 71.0 %copy-start.16 = (bf16[256,2048]{0,1:T(8,128)(2,1)}, bf16[256,2048]{0,1:T(8,128)(2,1)S(1)}, u32[]{:S(2)}) copy-start(bf16[256,2048]{0,1:T(8,128)(2,1)S(1)} %collective-permute-done.3) | copy-start | bytes 3145732
  523.2 23.3 %collective-permute-start.4 = (bf16[256,2048]{0,1:T(8,128)(2,1)S(1)}, bf16[256,2048]{0,1:T(8,128)(2,1)S(1)}, u32[]{:S(2)}, u32[]{:S(2)}) collective-permute-start(bf16[256,2048]{0,1:T(8,128)(2,1)S(1)} %collective-permute-done.3), channel_id=1, source_target_pairs={{0,2},{2,4},{4,6},{6,8},{8,10},{10,12},{12,14},{14,16},{16,18},{18... | collective-permute-start | bytes 3145736 | tf_op jit(solution)/shard_map/ppermute | solution.py:13
  546.5 47.6 %copy-start.17 = (bf16[256,2048]{0,1:T(8,128)(2,1)}, bf16[256,2048]{0,1:T(8,128)(2,1)S(1)}, u32[]{:S(2)}) copy-start(bf16[256,2048]{0,1:T(8,128)(2,1)S(1)} %collective-permute-done.4) | copy-start | bytes 3145732
  546.5 22.9 %collective-permute-start.5 = (bf16[256,2048]{0,1:T(8,128)(2,1)S(1)}, bf16[256,2048]{0,1:T(8,128)(2,1)S(1)}, u32[]{:S(2)}, u32[]{:S(2)}) collective-permute-start(bf16[256,2048]{0,1:T(8,128)(2,1)S(1)} %collective-permute-done.4), channel_id=1, source_target_pairs={{0,2},{2,4},{4,6},{6,8},{8,10},{10,12},{12,14},{14,16},{16,18},{18... | collective-permute-start | bytes 3145736 | tf_op jit(solution)/shard_map/ppermute | solution.py:13
  569.4 24.8 %copy-start.18 = (bf16[256,2048]{0,1:T(8,128)(2,1)}, bf16[256,2048]{0,1:T(8,128)(2,1)S(1)}, u32[]{:S(2)}) copy-start(bf16[256,2048]{0,1:T(8,128)(2,1)S(1)} %collective-permute-done.5) | copy-start | bytes 3145732
  569.4 24.8 %collective-permute-start.6 = (bf16[256,2048]{0,1:T(8,128)(2,1)S(1)}, bf16[256,2048]{0,1:T(8,128)(2,1)}, u32[]{:S(2)}, u32[]{:S(2)}) collective-permute-start(bf16[256,2048]{0,1:T(8,128)(2,1)S(1)} %collective-permute-done.5), channel_id=1, source_target_pairs={{0,2},{2,4},{4,6},{6,8},{8,10},{10,12},{12,14},{14,16},{16,18},{18... | collective-permute-start | bytes 3145736 | tf_op jit(solution)/shard_map/ppermute | solution.py:13
  594.1 33.0 %collective-permute-start.7 = (bf16[256,2048]{0,1:T(8,128)(2,1)}, bf16[256,2048]{0,1:T(8,128)(2,1)S(1)}, u32[]{:S(2)}, u32[]{:S(2)}) collective-permute-start(bf16[256,2048]{0,1:T(8,128)(2,1)} %collective-permute-done.6), channel_id=1, source_target_pairs={{0,2},{2,4},{4,6},{6,8},{8,10},{10,12},{12,14},{14,16},{16,18},{18... | collective-permute-start | bytes 3145736 | tf_op jit(solution)/shard_map/ppermute | solution.py:13
  600.8 26.3 %copy-start.13 = (bf16[256,2048]{0,1:T(8,128)(2,1)S(1)}, bf16[256,2048]{0,1:T(8,128)(2,1)}, u32[]{:S(2)}) copy-start(bf16[256,2048]{0,1:T(8,128)(2,1)} %copy-done.12) | copy-start | bytes 3145732
  636.7 48.4 %copy-start.22 = (bf16[2,1,128,2,16,64]{2,0,5,4,3,1:T(2,128)(2,1)S(1)}, bf16[2,1,128,2,16,64]{2,0,5,4,3,1:T(2,128)(2,1)}, u32[]{:S(2)}) copy-start(bf16[2,1,128,2,16,64]{2,0,5,4,3,1:T(2,128)(2,1)} %stack.226) | copy-start | bytes 3145732
  641.1 47.7 %copy-start.20 = (bf16[2,1,128,2,16,64]{2,0,5,4,3,1:T(2,128)(2,1)S(1)}, bf16[2,1,128,2,16,64]{2,0,5,4,3,1:T(2,128)(2,1)}, u32[]{:S(2)}) copy-start(bf16[2,1,128,2,16,64]{2,0,5,4,3,1:T(2,128)(2,1)} %stack.228) | copy-start | bytes 3145732
  650.0 31.4 %copy-start.24 = (bf16[2,1,128,2,16,64]{2,0,5,4,3,1:T(2,128)(2,1)S(1)}, bf16[2,1,128,2,16,64]{2,0,5,4,3,1:T(2,128)(2,1)}, u32[]{:S(2)}) copy-start(bf16[2,1,128,2,16,64]{2,0,5,4,3,1:T(2,128)(2,1)} %stack.224) | copy-start | bytes 3145732
  650.0 33.2 %copy-start.31 = (bf16[2,1,128,2,16,64]{2,0,5,4,3,1:T(2,128)(2,1)S(1)}, bf16[2,1,128,2,16,64]{2,0,5,4,3,1:T(2,128)(2,1)}, u32[]{:S(2)}) copy-start(bf16[2,1,128,2,16,64]{2,0,5,4,3,1:T(2,128)(2,1)} %stack.225) | copy-start | bytes 3145732
  650.0 36.9 %copy-start.29 = (bf16[2,1,128,2,16,64]{2,0,5,4,3,1:T(2,128)(2,1)S(1)}, bf16[2,1,128,2,16,64]{2,0,5,4,3,1:T(2,128)(2,1)}, u32[]{:S(2)}) copy-start(bf16[2,1,128,2,16,64]{2,0,5,4,3,1:T(2,128)(2,1)} %stack.227) | copy-start | bytes 3145732
  650.0 40.6 %copy-start.27 = (bf16[2,1,128,2,16,64]{2,0,5,4,3,1:T(2,128)(2,1)S(1)}, bf16[2,1,128,2,16,64]{2,0,5,4,3,1:T(2,128)(2,1)}, u32[]{:S(2)}) copy-start(bf16[2,1,128,2,16,64]{2,0,5,4,3,1:T(2,128)(2,1)} %stack.229) | copy-start | bytes 3145732
  715.1 12.6 %copy-start.32 = (bf16[2,128,2,16,64]{1,0,4,3,2:T(2,128)(2,1)S(1)}, bf16[2,128,2,16,64]{1,0,4,3,2:T(2,128)(2,1)}, u32[]{:S(2)}) copy-start(bf16[2,128,2,16,64]{1,0,4,3,2:T(2,128)(2,1)} %reshape.382) | copy-start | bytes 3145732
  1034.0 19.0 %copy-start.1 = (bf16[256,2048]{0,1:T(8,128)(2,1)S(1)}, bf16[256,2048]{0,1:T(8,128)(2,1)}, u32[]{:S(2)}) copy-start(bf16[256,2048]{0,1:T(8,128)(2,1)} %copy-done) | copy-start | bytes 3145732
  1034.0 19.1 %copy-start.3 = (bf16[256,2048]{0,1:T(8,128)(2,1)S(1)}, bf16[256,2048]{0,1:T(8,128)(2,1)}, u32[]{:S(2)}) copy-start(bf16[256,2048]{0,1:T(8,128)(2,1)} %copy-done.2) | copy-start | bytes 3145732
  (4 other events, 3.9 us)
Sparse Core Ops, SparseCore 0:
  1053.2 130.4 all-reduce.5
where the time goes:
time: 1210 us; the launch traced here: 1190 us
  local copies, waits for them, and re-layouts  602 us (50%)
  waiting for transfers between devices  415 us (34%)
  other arithmetic  72.7 us (6%)
  starting transfers between devices  50.3 us (4%)
  matrix products  37 us (3%)
  between operations  15 us (1%)
    ppermute x16, waiting for transfers between devices, passed_along(): return lax.ppermute(value, axis, pairs)  291 us
    rev x1, local copies, waits for them, and re-layouts, diagonal_taps(): flipped = grad_blocks[..., ::-1]  134 us
    unnamed x117, local copies, waits for them, and re-layouts  133 us
    psum x1, waiting for transfers between devices, per_device(): grad_filter = lax.psum(taps_grad, ('seq', 'head'))  124 us
    reshape x1, local copies, waits for them, and re-layouts, toeplitz_blocks(): sheared = sheared.reshape(filters, lags_count, block_len, 2 * block_len - 1)  60.3 us
    reshape x1, local copies, waits for them, and re-layouts, diagonal_taps(): sheared = flat.reshape(filters, lags_count, block_len, 2 * block_len - 1)  58.3 us
    ppermute x16, starting transfers between devices, passed_along(): return lax.ppermute(value, axis, pairs)  50.2 us
    reshape x1, local copies, waits for them, and re-layouts, diagonal_taps(): flat = padded.reshape(filters, lags_count, 2 * block_len * block_len)  38.1 us
  transfers between devices with their start and end apart: 17, of which 15 were waited for; matrix products, arithmetic and copies ran while one was open for 14% of the time, Pallas kernels for 0%

commit v1 on v0

v1 whole, which is shorter than its diff:
```python
import functools

import jax
import jax.numpy as jnp
from jax import lax
from jax.experimental import pallas as pl
from jax.experimental.pallas import tpu as pltpu
from jax.sharding import PartitionSpec as P

DH = 64
BLK = 128
MOST = 12
RANKS = 4
QUANTUM = 4
MESH = pl.DeviceIdType.MESH
ANY = pl.BlockSpec(memory_space=pl.ANY)


def wide(ref):
    return ref[...].astype(jnp.float32)


def prepare_kernel(groups, *refs):
    value, key = refs[:groups], refs[groups : 2 * groups]
    query, cot = refs[2 * groups : 3 * groups], refs[3 * groups : 4 * groups]
    product_ref, scaled_ref = refs[4 * groups :]
    for left, right, out in ((value, key, product_ref), (query, cot, scaled_ref)):
        parts = [wide(a) * wide(b) for a, b in zip(left, right)]
        for f in range(out.shape[0]):
            piece = jnp.concatenate([part[:, f * DH : (f + 1) * DH] for part in parts], 1)
            out[f] = piece.astype(jnp.bfloat16)


def prepare(value_rows, key_rows, query_rows, cotangent, filters):
    rows, channels = value_rows.shape
    groups = channels // (filters * DH)
    width = 4 * DH
    steps = filters // 4

    def spec(g):
        return pl.BlockSpec((rows, width), lambda p: (0, g * steps + p))

    specs = [spec(g) for g in range(groups)]
    args = []
    for array in (value_rows, key_rows, query_rows, cotangent):
        args += [array] * groups
    out = jax.ShapeDtypeStruct((filters, rows, groups * DH), jnp.bfloat16)
    out_spec = pl.BlockSpec((4, rows, groups * DH), lambda p: (p, 0, 0))
    return pl.pallas_call(
        functools.partial(prepare_kernel, groups),
        grid=(steps,),
        in_specs=specs * 4,
        out_specs=[out_spec, out_spec],
        out_shape=[out, out],
        compiler_params=pltpu.CompilerParams(vmem_limit_bytes=32 << 20),
    )(*args)


def finish_kernel(groups, conv, adj, value, key, query, cot, out, gq, gk, gv):
    for g in range(groups):

        @pl.when(pl.program_id(1) == g)
        def _():
            def joined(ref):
                parts = [
                    ref[f].astype(jnp.float32)[:, g * DH : (g + 1) * DH]
                    for f in range(ref.shape[0])
                ]
                return jnp.concatenate(parts, 1)

            convolved, adjoint = joined(conv), joined(adj)
            out[...] = (wide(query) * convolved).astype(jnp.bfloat16)
            gq[...] = (wide(cot) * convolved).astype(jnp.bfloat16)
            gk[...] = (wide(value) * adjoint).astype(jnp.bfloat16)
            gv[...] = (wide(key) * adjoint).astype(jnp.bfloat16)


def finish(conv, adj, value_rows, key_rows, query_rows, cotangent):
    filters, rows, cols = conv.shape
    groups = cols // DH
    steps = filters // 4
    spec = pl.BlockSpec((rows, 4 * DH), lambda p, g: (0, g * steps + p))
    back = pl.BlockSpec((4, rows, cols), lambda p, g: (p, 0, 0))
    shape = jax.ShapeDtypeStruct(value_rows.shape, jnp.bfloat16)
    return pl.pallas_call(
        functools.partial(finish_kernel, groups),
        grid=(steps, groups),
        in_specs=[back, back, spec, spec, spec, spec],
        out_specs=[spec] * 4,
        out_shape=[shape] * 4,
        compiler_params=pltpu.CompilerParams(vmem_limit_bytes=32 << 20),
    )(conv, adj, value_rows, key_rows, query_rows, cotangent)


def halo_parts(own, reach):
    parts, left, step = [], reach, 1
    while left > 0:
        parts.append((step, min(own, left)))
        left -= min(own, left)
        step += 1
    return parts


def spread_kernel(teams, reach, prod, scal, past, future, sends, recvs, far_sends, far_recvs, local_sems):
    per_rank, rows = prod.shape[1], prod.shape[2]
    own = RANKS * rows
    me = lax.axis_index("seq")
    rank, team = lax.rem(me, RANKS), lax.div(me, RANKS)
    halos = halo_parts(own, reach)
    barrier = pltpu.get_barrier_semaphore()
    peers = [team * RANKS + lax.rem(rank + k, RANKS) for k in range(1, RANKS)]
    for peer in peers:
        pl.semaphore_signal(barrier, inc=1, device_id={"seq": peer}, device_id_type=MESH)
    for k in range(1, teams):
        other = lax.rem(team + k, teams) * RANKS + rank
        pl.semaphore_signal(barrier, inc=1, device_id={"seq": other}, device_id_type=MESH)
    pl.semaphore_wait(barrier, RANKS + teams - 2)

    arrays = ((prod, past, reach), (scal, future, 0))
    at = pl.multiple_of(rank * rows, rows)

    def near(a, f, k):
        source, target, base = arrays[a]
        to = lax.rem(rank + k, RANKS)
        return pltpu.make_async_remote_copy(
            src_ref=source.at[to, f],
            dst_ref=target.at[f, pl.ds(base + at, rows)],
            send_sem=sends.at[a, f, k - 1],
            recv_sem=recvs.at[a, f, k - 1],
            device_id={"seq": team * RANKS + to},
            device_id_type=MESH,
        )

    def local(a, f):
        source, target, base = arrays[a]
        return pltpu.make_async_copy(
            source.at[rank, f], target.at[f, pl.ds(base + at, rows)], local_sems.at[a, f]
        )

    def far(a, f, h):
        step, size = halos[h]
        target = arrays[a][1]
        if a == 0:
            start = reach - (step - 1) * own - size
            src, dst, other = pl.ds(reach + own - size, size), pl.ds(start, size), me + step * RANKS
        else:
            src, dst, other = pl.ds(0, size), pl.ds(step * own, size), me - step * RANKS
        return pltpu.make_async_remote_copy(
            src_ref=target.at[f, src],
            dst_ref=target.at[f, dst],
            send_sem=far_sends.at[a, f, h],
            recv_sem=far_recvs.at[a, f, h],
            device_id={"seq": other},
            device_id_type=MESH,
        )

    def gives(a, h):
        step = halos[h][0]
        return team + step < teams if a == 0 else team - step >= 0

    def takes(a, h):
        step = halos[h][0]
        return team - step >= 0 if a == 0 else team + step < teams

    for f in range(per_rank):
        for a in range(2):
            local(a, f).start()
            for k in range(1, RANKS):
                near(a, f, k).start()
    for f in range(per_rank):
        for a in range(2):
            local(a, f).wait()
            for k in range(1, RANKS):
                near(a, f, k).wait_recv()
            for h in range(len(halos)):
                pl.when(gives(a, h))(lambda: far(a, f, h).start())
    for f in range(per_rank):
        for a in range(2):
            for k in range(1, RANKS):
                near(a, f, k).wait_send()
            for h in range(len(halos)):
                pl.when(gives(a, h))(lambda: far(a, f, h).wait_send())
                pl.when(takes(a, h))(lambda: far(a, f, h).wait_recv())


def spread(product, scaled, teams, reach):
    _, per_rank, rows, cols = product.shape
    out = jax.ShapeDtypeStruct((per_rank, RANKS * rows + reach, cols), jnp.bfloat16)
    halos = len(halo_parts(RANKS * rows, reach))
    return pl.pallas_call(
        functools.partial(spread_kernel, teams, reach),
        in_specs=[ANY, ANY],
        out_specs=[ANY, ANY],
        out_shape=[out, out],
        scratch_shapes=[
            pltpu.SemaphoreType.DMA((2, per_rank, RANKS - 1)),
            pltpu.SemaphoreType.DMA((2, per_rank, RANKS - 1)),
            pltpu.SemaphoreType.DMA((2, per_rank, halos)),
            pltpu.SemaphoreType.DMA((2, per_rank, halos)),
            pltpu.SemaphoreType.DMA((2, per_rank)),
        ],
        compiler_params=pltpu.CompilerParams(collective_id=0, has_side_effects=True),
    )(product, scaled)


def mix_kernel(back_len, fore_len, past_taps, fore_taps, past, future, conv, adj, grad, tp, tf, g_ref):
    cols = past.shape[2]
    own = conv.shape[1]
    reach = past.shape[1] - own
    span = tp.shape[1]
    lags = reach // BLK + 1
    for taps, strip in ((past_taps, tp), (fore_taps, tf)):
        rows = jnp.broadcast_to(taps[0], (BLK, span))
        strip[...] = pltpu.roll(rows, 0, 1, stride=1, stride_axis=0).astype(jnp.bfloat16)
    g_ref[...] = jnp.zeros_like(g_ref)
    i0 = lax.broadcasted_iota(jnp.int32, (BLK, BLK), 0)
    i1 = lax.broadcasted_iota(jnp.int32, (BLK, BLK), 1)
    mirror = (i0 + i1 == BLK - 1).astype(jnp.bfloat16)

    @pl.loop(0, own // BLK)
    def _(n):
        row = pl.multiple_of(n * BLK, BLK)
        lb, lf = back_len[n], fore_len[n]
        turned = jnp.dot(
            mirror, future[0, pl.ds(row, BLK)], preferred_element_type=jnp.float32
        ).astype(jnp.bfloat16)
        for size in range(QUANTUM, lags + 1, QUANTUM):
            wide_by = size * BLK
            at = lax.broadcasted_iota(jnp.int32, (wide_by, cols), 0)

            @pl.when((lb <= size) & (lb > size - QUANTUM))
            def _():
                first = pl.multiple_of(row + reach + BLK - wide_by, BLK)
                x = past[0, pl.ds(first, wide_by)]
                x = jnp.where(at >= (size - lb) * BLK, x, jnp.zeros_like(x))
                low = (lags - size) * BLK
                sums = jnp.dot(
                    tp[:, low : lags * BLK], x, preferred_element_type=jnp.float32
                )
                conv[0, pl.ds(row, BLK)] = sums.astype(jnp.bfloat16)
                g_ref[:, low : lags * BLK] += lax.dot_general(
                    turned, x, (((1,), (1,)), ((), ())), preferred_element_type=jnp.float32
                )

            @pl.when((lf <= size) & (lf > size - QUANTUM))
            def _():
                x = future[0, pl.ds(row, wide_by)]
                x = jnp.where(at < lf * BLK, x, jnp.zeros_like(x))
                sums = jnp.dot(tf[:, :wide_by], x, preferred_element_type=jnp.float32)
                adj[0, pl.ds(row, BLK)] = sums.astype(jnp.bfloat16)

    aligned = pltpu.roll(g_ref[...], 0, 1, stride=1, stride_axis=0)
    grad[0] = jnp.sum(aligned, 0, keepdims=True)


def mix(back_len, fore_len, past_taps, fore_taps, past, future, own):
    per_rank, rows, cols = past.shape
    span = past_taps.shape[2]

    def spec(*dims):
        return pl.BlockSpec((1,) + dims, lambda f, *_: (f, 0, 0))

    out = jax.ShapeDtypeStruct((per_rank, own, cols), jnp.bfloat16)
    return pl.pallas_call(
        mix_kernel,
        grid_spec=pltpu.PrefetchScalarGridSpec(
            num_scalar_prefetch=2,
            grid=(per_rank,),
            in_specs=[spec(1, span), spec(1, span), spec(rows, cols), spec(rows, cols)],
            out_specs=[spec(own, cols), spec(own, cols), spec(1, span)],
            scratch_shapes=[
                pltpu.VMEM((BLK, span), jnp.bfloat16),
                pltpu.VMEM((BLK, span), jnp.bfloat16),
                pltpu.VMEM((BLK, span), jnp.float32),
            ],
        ),
        out_shape=[out, out, jax.ShapeDtypeStruct((per_rank, 1, span), jnp.float32)],
        compiler_params=pltpu.CompilerParams(vmem_limit_bytes=48 << 20),
    )(back_len, fore_len, past_taps, fore_taps, past, future)


def gather_kernel(teams, heads, conv, adj, grad, conv_all, adj_all, grad_all, slots, sends, recvs, g_sends, g_recvs, s_sends, s_recvs, local_sems):
    rows = conv_all.shape[2]
    me, head = lax.axis_index("seq"), lax.axis_index("head")
    rank, team = lax.rem(me, RANKS), lax.div(me, RANKS)
    barrier = pltpu.get_barrier_semaphore()
    ring = [(t, h) for t in range(teams) for h in range(heads)][1:]

    def mate(t, h):
        return {
            "seq": lax.rem(team + t, teams) * RANKS + rank,
            "head": lax.rem(head + h, heads),
        }

    def near_id(k):
        return {"seq": team * RANKS + lax.rem(rank + k, RANKS), "head": head}

    for k in range(1, RANKS):
        pl.semaphore_signal(barrier, inc=1, device_id=near_id(k), device_id_type=MESH)
    for t, h in ring:
        pl.semaphore_signal(barrier, inc=1, device_id=mate(t, h), device_id_type=MESH)
    pl.semaphore_wait(barrier, RANKS - 1 + len(ring))

    def sum_copy(i):
        return pltpu.make_async_remote_copy(
            src_ref=grad,
            dst_ref=slots.at[i],
            send_sem=g_sends.at[i],
            recv_sem=g_recvs.at[i],
            device_id=mate(*ring[i]),
            device_id_type=MESH,
        )

    def near(a, k):
        source, target = ((conv, conv_all), (adj, adj_all))[a]
        to = lax.rem(rank + k, RANKS)
        return pltpu.make_async_remote_copy(
            src_ref=source.at[:, pl.ds(pl.multiple_of(to * rows, rows), rows)],
            dst_ref=target.at[rank],
            send_sem=sends.at[a, k - 1],
            recv_sem=recvs.at[a, k - 1],
            device_id=near_id(k),
            device_id_type=MESH,
        )

    def local(a):
        source, target = ((conv, conv_all), (adj, adj_all))[a]
        return pltpu.make_async_copy(
            source.at[:, pl.ds(pl.multiple_of(rank * rows, rows), rows)],
            target.at[rank],
            local_sems.at[a],
        )

    def share(k):
        return pltpu.make_async_remote_copy(
            src_ref=grad_all.at[rank],
            dst_ref=grad_all.at[rank],
            send_sem=s_sends.at[k - 1],
            recv_sem=s_recvs.at[k - 1],
            device_id=near_id(k),
            device_id_type=MESH,
        )

    for i in range(len(ring)):
        sum_copy(i).start()
    for a in range(2):
        local(a).start()
        for k in range(1, RANKS):
            near(a, k).start()
    total = grad[...]
    for i in range(len(ring)):
        sum_copy(i).wait_recv()
    for i in range(len(ring)):
        total = total + slots[i]
    grad_all[rank] = total
    for k in range(1, RANKS):
        share(k).start()
    for i in range(len(ring)):
        sum_copy(i).wait_send()
    for a in range(2):
        local(a).wait()
        for k in range(1, RANKS):
            near(a, k).wait()
    for k in range(1, RANKS):
        share(k).wait()


def gather(conv, adj, grad, teams, heads):
    per_rank, own, cols = conv.shape
    out = jax.ShapeDtypeStruct((RANKS, per_rank, own // RANKS, cols), jnp.bfloat16)
    others = teams * heads - 1
    vmem = pl.BlockSpec(memory_space=pltpu.VMEM)
    dma = pltpu.SemaphoreType.DMA
    return pl.pallas_call(
        functools.partial(gather_kernel, teams, heads),
        in_specs=[ANY, ANY, vmem],
        out_specs=[ANY, ANY, vmem],
        out_shape=[out, out, jax.ShapeDtypeStruct((RANKS,) + grad.shape, jnp.float32)],
        scratch_shapes=[
            pltpu.VMEM((others,) + grad.shape, jnp.float32),
            dma((2, RANKS - 1)),
            dma((2, RANKS - 1)),
            dma((others,)),
            dma((others,)),
            dma((RANKS - 1,)),
            dma((RANKS - 1,)),
            dma((2,)),
        ],
        compiler_params=pltpu.CompilerParams(
            collective_id=1, has_side_effects=True, vmem_limit_bytes=32 << 20
        ),
    )(conv, adj, grad)


def per_device(value_rows, key_rows, query_rows, cotangent, filter_taps, doc_blocks):
    rows, channels = value_rows.shape
    filters, taps_total = filter_taps.shape
    cols = channels // filters
    per_rank = filters // RANKS
    seq, heads = lax.axis_size("seq"), lax.axis_size("head")
    teams = seq // RANKS
    own = RANKS * rows
    own_blocks = own // BLK
    lags = min(MOST, taps_total // BLK)
    reach = (lags - 1) * BLK
    used = lags * BLK
    me = lax.axis_index("seq")
    rank, team = lax.rem(me, RANKS), lax.div(me, RANKS)

    product, scaled = prepare(value_rows, key_rows, query_rows, cotangent, filters)
    shape = (RANKS, per_rank, rows, cols)
    past, future = spread(product.reshape(shape), scaled.reshape(shape), teams, reach)

    mine = lax.dynamic_slice_in_dim(filter_taps, rank * per_rank, per_rank, 0)[:, :used]
    mine = mine.astype(jnp.bfloat16).astype(jnp.float32)
    turned = mine[:, ::-1]
    gap = jnp.zeros((per_rank, BLK), jnp.float32)
    past_taps = jnp.concatenate([turned[:, BLK - 1 :], gap, turned[:, : BLK - 1]], 1)
    fore_taps = jnp.concatenate([mine, gap], 1)

    fill = jnp.full((lags - 1,), -1, jnp.int32)
    docs = jnp.concatenate([fill, doc_blocks, fill - 1], 0)
    window = lax.dynamic_slice_in_dim(docs, team * own_blocks, own_blocks + 2 * (lags - 1))
    here = window[lags - 1 : lags - 1 + own_blocks]
    back_len = sum(
        (window[lags - 1 - b : lags - 1 - b + own_blocks] == here).astype(jnp.int32)
        for b in range(lags)
    )
    fore_len = sum(
        (window[lags - 1 + b : lags - 1 + b + own_blocks] == here).astype(jnp.int32)
        for b in range(lags)
    )
    conv, adj, grad = mix(
        back_len, fore_len, past_taps[:, None], fore_taps[:, None], past, future, own
    )
    conv_all, adj_all, grad_all = gather(
        conv, adj, jnp.pad(grad[:, 0, :used], ((0, 0), (0, taps_total - used))).reshape(-1, BLK),
        teams, heads,
    )
    whole = (filters, rows, cols)
    outs = finish(
        conv_all.reshape(whole), adj_all.reshape(whole), value_rows, key_rows, query_rows, cotangent
    )
    taps_grad = grad_all.reshape(filters, taps_total)[:, :used][:, ::-1]
    taps_grad = jnp.pad(taps_grad, ((0, 0), (0, taps_total - used)))
    return (*outs, taps_grad * (1.0 / (rows * seq)))


def solution(mesh):
    rows = P("seq", "head")
    return jax.shard_map(
        per_device,
        mesh=mesh,
        in_specs=(rows, rows, rows, rows, P(), P()),
        out_specs=(rows, rows, rows, rows, P()),
        check_vma=False,
    )
```

time: 1210 us -> 138 us (0.11); the launches traced: 1190 us -> 138 us
  local copies, waits for them, and re-layouts: 602 us -> 21.1 us
  waiting for transfers between devices: 415 us -> 0 us
  Pallas kernels: 0 us -> 114 us
  other arithmetic: 72.7 us -> 2.4 us
  starting transfers between devices: 50.3 us -> 0 us
  matrix products: 37 us -> 0 us
  between operations: 15 us -> 0.84 us
    ppermute x16 -> x0, waiting for transfers between devices: 291 us -> none  [passed_along(): return lax.ppermute(value, axis, pairs)]
    reshape x7 -> x2, local copies, waits for them, and re-layouts: 185 us -> 0.05 us  [the longest x1 0.03 us: per_device(): taps_grad = grad_all.reshape(filters, taps_total)[:, :used][:, ::-1]]
    rev x1, local copies, waits for them, and re-layouts: 134 us -> 0.87 us  [per_device(): taps_grad = grad_all.reshape(filters, taps_total)[:, :used][:, ::-1]]
    psum x1 -> x0, waiting for transfers between devices: 124 us -> none  [per_device(): grad_filter = lax.psum(taps_grad, ('seq', 'head'))]
    pallas_call x0 -> x5, Pallas kernels: none -> 114 us  [the longest x1 53.7 us: spread(): pl.pallas_call(functools.partial(spread_kernel, teams, reach), in_specs=[...]
    unnamed x117 -> x41, local copies, waits for them, and re-layouts: 133 us -> 19.8 us
    another operation x73 -> x2, local copies, waits for them, and re-layouts: 75.2 us -> 0.01 us  [the longest x18 36.1 us: per_device(): jnp.stack([past_blocks[margin - b:margin - b + blocks_dev] for b in range...]
    ppermute x16 -> x0, starting transfers between devices: 50.2 us -> none  [passed_along(): return lax.ppermute(value, axis, pairs)]
  transfers between devices with their start and end apart: 17 -> 0, of which waited for: 15 -> 0; matrix products, arithmetic and copies ran while one was open for 14% -> 0% of each run, Pallas kernels for 0% -> 0%
where the time goes in v1:
time: 138 us
  Pallas kernels  114 us (83%)
  local copies, waits for them, and re-layouts  21.1 us (15%)
  other arithmetic  2.4 us (2%)
    pallas_call x1, Pallas kernels, spread(): pl.pallas_call(functools.partial(spread_kernel, teams, reach), in_specs=[...  53.7 us
    pallas_call x1, Pallas kernels, gather(): pl.pallas_call(functools.partial(gather_kernel, teams, heads), in_specs=[...  30.4 us
    pallas_call x1, Pallas kernels, mix(): pl.pallas_call(mix_kernel, grid_spec=pltpu.PrefetchScalarGridSpec(num_sca...  23.3 us
    unnamed x41, local copies, waits for them, and re-layouts  19.8 us
    pallas_call x1, Pallas kernels, finish(): pl.pallas_call(functools.partial(finish_kernel, groups), grid=(steps, gro...  4.76 us

profile of v1, /device:TPU:0, one launch (start us, length us, event | category | flops | bytes accessed | tf_op | source)
XLA Modules:
  0.0 138.2 jit_solution(798310252944456092)
XLA Ops:
  0.7 0.7 pad_add_fusion
  1.4 0.1 dynamic_slice.6
  1.5 0.1 fusion.22.fore_len
  1.6 0.1 fusion.11.back_len
  1.7 0.8 fusion
  2.5 0.1 slice.124
  2.5 0.1 slice.120
  2.6 1.0 reverse.2
  3.7 0.1 slice.162
  3.8 0.1 concatenate.10
  4.0 0.0 copy-start
  4.0 1.2 copy-done
  5.2 0.0 copy-start.2
  5.2 1.2 copy-done.2
  6.4 0.0 copy-start.4
  6.4 1.2 copy-done.4
  7.6 0.0 copy-start.6
  7.6 1.2 copy-done.6
  8.9 1.7 %shard_map.101 = (bf16[16,256,128]{2,1,0:T(8,128)(2,1)S(1)}, bf16[16,256,128]{2,1,0:T(8,128)(2,1)S(1)}) custom-call(bf16[256,2048]{1,0:T(8,128)(2,1)S(1)} %copy-done, bf16[256,2048]{1,0:T(8,128)(2,1)S(1)} %copy-done, bf16[256,2048]{1,0:T(8,128)(2,1)S(1)} %copy-done.2, bf16[256,2048]{1,0:T(8,128)(2,1)S(1)} %copy-done.2, bf16[256,2048]{1,0:T(8,128)(2,1)S(1)} %copy-done.4, ...), custom_call_target="tpu_custom_call" | custom-call | tf_op jit(solution)/shard_map/pallas_call | solution.py:49
  10.6 0.0 copy-start.13
  10.6 1.0 copy-done.13
  11.6 0.0 copy-start.14
  11.6 1.0 copy-done.14
  12.5 53.7 %shard_map.102 = (bf16[4,2432,128]{2,1,0:T(8,128)(2,1)}, bf16[4,2432,128]{2,1,0:T(8,128)(2,1)}) custom-call(bf16[4,4,256,128]{3,2,1,0:T(8,128)(2,1)} %bitcast.10, bf16[4,4,256,128]{3,2,1,0:T(8,128)(2,1)} %bitcast.11), custom_call_target="tpu_custom_call" | custom-call | tf_op jit(solution)/shard_map/pallas_call | solution.py:190
  66.2 0.0 copy-start.8
  66.2 1.7 %copy-done.8 = bf16[4,2432,128]{2,1,0:T(8,128)(2,1)S(1)} copy-done((bf16[4,2432,128]{2,1,0:T(8,128)(2,1)S(1)}, bf16[4,2432,128]{2,1,0:T(8,128)(2,1)}, u32[]{:S(2)}) %copy-start.8) | copy-done | bytes 2490392
  67.9 23.3 %shard_map.103 = (bf16[4,1024,128]{2,1,0:T(8,128)(2,1)S(1)}, bf16[4,1024,128]{2,1,0:T(8,128)(2,1)S(1)}, f32[4,1,1664]{2,1,0:T(1,128)S(1)}) custom-call(s32[8]{0:T(128)S(1)} %fusion.11.back_len, s32[8]{0:T(128)S(1)} %fusion.22.fore_len, f32[4,1,1664]{2,1,0:T(1,128)S(1)} %copy.11.past_taps, f32[4,1,1664]{2,1,0:T(1,128)S(1)} %broadcast_in_dim.11.fore_taps, ...), custom_call_target="tpu_custom_call" | custom-call | tf_op jit(solution)/shard_map/pallas_call | solution.py:264
  91.2 0.0 copy-start.9
  91.2 1.0 copy-done.9
  92.2 0.0 copy-start.11
  92.2 1.0 copy-done.11
  93.2 0.0 copy-start.1
  93.2 0.0 copy-start.10
  93.3 1.4 copy-done.10
  94.6 1.2 copy-done.12
  95.8 30.4 %shard_map.104 = (bf16[4,4,256,128]{3,2,1,0:T(8,128)(2,1)S(1)}, bf16[4,4,256,128]{3,2,1,0:T(8,128)(2,1)S(1)}, f32[4,64,128]{2,1,0:T(8,128)S(1)}) custom-call(bf16[4,1024,128]{2,1,0:T(8,128)(2,1)S(1)} %copy-done.10, bf16[4,1024,128]{2,1,0:T(8,128)(2,1)S(1)} %copy-done.12, f32[64,128]{1,0:T(8,128)S(1)} %reshape.30.grad), custom_call_target="tpu_custom_call" | custom-call | tf_op jit(solution)/shard_map/pallas_call | solution.py:374
  126.2 0.0 copy-start.15
  126.2 1.0 copy-done.15
  127.2 1.0 copy-done.17
  128.2 0.9 rev.4
  129.1 0.7 pad_multiply_fusion
  129.8 0.0 copy-done.1
  129.8 0.0 copy-done.3
  129.8 0.0 copy-done.5
  129.8 1.2 copy-done.7
  131.0 1.2 copy-done.16
  132.2 1.2 copy-done.18
  133.5 4.8 %shard_map.105 = (bf16[256,2048]{1,0:T(8,128)(2,1)}, bf16[256,2048]{1,0:T(8,128)(2,1)}, bf16[256,2048]{1,0:T(8,128)(2,1)}, bf16[256,2048]{1,0:T(8,128)(2,1)}) custom-call(bf16[16,256,128]{2,1,0:T(8,128)(2,1)S(1)} %bitcast.12, bf16[16,256,128]{2,1,0:T(8,128)(2,1)S(1)} %bitcast.13, bf16[256,2048]{1,0:T(8,128)(2,1)S(1)} %copy-done.1, ...), custom_call_target="tpu_custom_call" | custom-call | tf_op jit(solution)/shard_map/pallas_call | solution.py:85
  (19 shorter events, 0.2 us)
Async XLA Ops:
  4.0 1.2 copy-start
  5.2 1.2 copy-start.2
  6.4 1.2 copy-start.4
  7.6 1.2 copy-start.6
  10.6 1.0 copy-start.13
  11.6 1.0 copy-start.14
  66.2 1.7 %copy-start.8 = (bf16[4,2432,128]{2,1,0:T(8,128)(2,1)S(1)}, bf16[4,2432,128]{2,1,0:T(8,128)(2,1)}, u32[]{:S(2)}) copy-start(bf16[4,2432,128]{2,1,0:T(8,128)(2,1)} %get-tuple-element.21.past) | copy-start | bytes 7471108
  91.2 1.0 copy-start.9
  92.2 1.0 copy-start.11
  93.2 36.6 %copy-start.1 = (bf16[256,2048]{1,0:T(8,128)(2,1)S(1)}, bf16[256,2048]{1,0:T(8,128)(2,1)}, u32[]{:S(2)}) copy-start(bf16[256,2048]{1,0:T(8,128)(2,1)} %value.1) | copy-start | bytes 3145732
  93.2 36.6 %copy-start.3 = (bf16[256,2048]{1,0:T(8,128)(2,1)S(1)}, bf16[256,2048]{1,0:T(8,128)(2,1)}, u32[]{:S(2)}) copy-start(bf16[256,2048]{1,0:T(8,128)(2,1)} %key.1) | copy-start | bytes 3145732
  93.2 36.6 %copy-start.5 = (bf16[256,2048]{1,0:T(8,128)(2,1)S(1)}, bf16[256,2048]{1,0:T(8,128)(2,1)}, u32[]{:S(2)}) copy-start(bf16[256,2048]{1,0:T(8,128)(2,1)} %query.1) | copy-start | bytes 3145732
  93.2 1.4 copy-start.10
  94.6 1.2 copy-start.12
  126.2 1.0 copy-start.15
  127.2 1.0 copy-start.17
  129.8 1.2 copy-start.7
  131.0 1.2 copy-start.16
  132.2 1.2 copy-start.18

commit v2 on v1

v2 whole, which is shorter than its diff:
```python
import functools

import jax
import jax.numpy as jnp
from jax import lax
from jax.experimental import pallas as pl
from jax.experimental.pallas import tpu as pltpu
from jax.sharding import PartitionSpec as P

DH = 64
BLK = 128
MOST = 12
RANKS = 4
MESH = pl.DeviceIdType.MESH
ANY = pl.BlockSpec(memory_space=pl.ANY)


def wide(ref):
    return ref[...].astype(jnp.float32)


def prepare_kernel(groups, *refs):
    value, key = refs[:groups], refs[groups : 2 * groups]
    query, cot = refs[2 * groups : 3 * groups], refs[3 * groups : 4 * groups]
    product_ref, scaled_ref = refs[4 * groups :]
    for left, right, out in ((value, key, product_ref), (query, cot, scaled_ref)):
        parts = [wide(a) * wide(b) for a, b in zip(left, right)]
        for f in range(out.shape[0]):
            piece = jnp.concatenate([part[:, f * DH : (f + 1) * DH] for part in parts], 1)
            out[f] = piece.astype(jnp.bfloat16)


def prepare(value_rows, key_rows, query_rows, cotangent, filters):
    rows, channels = value_rows.shape
    groups = channels // (filters * DH)
    width = 4 * DH
    steps = filters // 4

    def spec(g):
        return pl.BlockSpec((rows, width), lambda p: (0, g * steps + p))

    specs = [spec(g) for g in range(groups)]
    args = []
    for array in (value_rows, key_rows, query_rows, cotangent):
        args += [array] * groups
    out = jax.ShapeDtypeStruct((filters, rows, groups * DH), jnp.bfloat16)
    out_spec = pl.BlockSpec((4, rows, groups * DH), lambda p: (p, 0, 0))
    return pl.pallas_call(
        functools.partial(prepare_kernel, groups),
        grid=(steps,),
        in_specs=specs * 4,
        out_specs=[out_spec, out_spec],
        out_shape=[out, out],
        compiler_params=pltpu.CompilerParams(vmem_limit_bytes=56 << 20),
    )(*args)


def finish_kernel(groups, conv, adj, value, key, query, cot, out, gq, gk, gv):
    for g in range(groups):

        @pl.when(pl.program_id(1) == g)
        def _():
            def joined(ref):
                parts = [
                    ref[f].astype(jnp.float32)[:, g * DH : (g + 1) * DH]
                    for f in range(ref.shape[0])
                ]
                return jnp.concatenate(parts, 1)

            convolved, adjoint = joined(conv), joined(adj)
            out[...] = (wide(query) * convolved).astype(jnp.bfloat16)
            gq[...] = (wide(cot) * convolved).astype(jnp.bfloat16)
            gk[...] = (wide(value) * adjoint).astype(jnp.bfloat16)
            gv[...] = (wide(key) * adjoint).astype(jnp.bfloat16)


def finish(conv, adj, value_rows, key_rows, query_rows, cotangent):
    filters, rows, cols = conv.shape
    groups = cols // DH
    steps = filters // 4
    spec = pl.BlockSpec((rows, 4 * DH), lambda p, g: (0, g * steps + p))
    back = pl.BlockSpec((4, rows, cols), lambda p, g: (p, 0, 0))
    shape = jax.ShapeDtypeStruct(value_rows.shape, jnp.bfloat16)
    return pl.pallas_call(
        functools.partial(finish_kernel, groups),
        grid=(steps, groups),
        in_specs=[back, back, spec, spec, spec, spec],
        out_specs=[spec] * 4,
        out_shape=[shape] * 4,
        compiler_params=pltpu.CompilerParams(vmem_limit_bytes=56 << 20),
    )(conv, adj, value_rows, key_rows, query_rows, cotangent)


def halo_parts(own, reach):
    parts, left, step = [], reach, 1
    while left > 0:
        parts.append((step, min(own, left)))
        left -= min(own, left)
        step += 1
    return parts


def mix_kernel(
    teams, heads, reach, back_len, fore_len, past_taps, fore_taps, prod, scal,
    conv_all, adj_all, grad_all,
    past, future, tp, tf, g_ref, conv, adj, grad, slots,
    sends, recvs, far_sends, far_recvs, out_sends, out_recvs, g_sends, g_recvs, s_sends, s_recvs,
    local_sems, out_local,
):
    _, per_rank, rows, cols = prod.shape
    own = RANKS * rows
    span = tp.shape[2]
    used = span - BLK
    lines = grad.shape[1]
    me, head = lax.axis_index("seq"), lax.axis_index("head")
    rank, team = lax.rem(me, RANKS), lax.div(me, RANKS)
    halos = halo_parts(own, reach)
    ring = [(t, h) for t in range(teams) for h in range(heads)][1:]
    arrays = ((prod, past, reach), (scal, future, 0))
    returns = ((conv, conv_all), (adj, adj_all))
    at = pl.multiple_of(rank * rows, rows)

    def mate(t, h):
        return {
            "seq": lax.rem(team + t, teams) * RANKS + rank,
            "head": lax.rem(head + h, heads),
        }

    def near_id(k):
        return {"seq": team * RANKS + lax.rem(rank + k, RANKS), "head": head}

    barrier = pltpu.get_barrier_semaphore()
    for k in range(1, RANKS):
        pl.semaphore_signal(barrier, inc=1, device_id=near_id(k), device_id_type=MESH)
    for t, h in ring:
        pl.semaphore_signal(barrier, inc=1, device_id=mate(t, h), device_id_type=MESH)
    pl.semaphore_wait(barrier, RANKS - 1 + len(ring))

    def near(a, f, k):
        source, target, base = arrays[a]
        return pltpu.make_async_remote_copy(
            src_ref=source.at[lax.rem(rank + k, RANKS), f],
            dst_ref=target.at[f, pl.ds(base + at, rows)],
            send_sem=sends.at[a, f, k - 1],
            recv_sem=recvs.at[a, f, k - 1],
            device_id=near_id(k),
            device_id_type=MESH,
        )

    def local(a, f):
        source, target, base = arrays[a]
        return pltpu.make_async_copy(
            source.at[rank, f], target.at[f, pl.ds(base + at, rows)], local_sems.at[a, f]
        )

    def far(a, f, h):
        step, size = halos[h]
        target = arrays[a][1]
        if a == 0:
            start = reach - (step - 1) * own - size
            src, dst, other = pl.ds(reach + own - size, size), pl.ds(start, size), me + step * RANKS
        else:
            src, dst, other = pl.ds(0, size), pl.ds(step * own, size), me - step * RANKS
        return pltpu.make_async_remote_copy(
            src_ref=target.at[f, src],
            dst_ref=target.at[f, dst],
            send_sem=far_sends.at[a, f, h],
            recv_sem=far_recvs.at[a, f, h],
            device_id={"seq": other, "head": head},
            device_id_type=MESH,
        )

    def gives(a, h):
        step = halos[h][0]
        return team + step < teams if a == 0 else team - step >= 0

    def takes(a, h):
        step = halos[h][0]
        return team - step >= 0 if a == 0 else team + step < teams

    def back(a, f, k):
        source, target = returns[a]
        to = lax.rem(rank + k, RANKS)
        return pltpu.make_async_remote_copy(
            src_ref=source.at[f, pl.ds(pl.multiple_of(to * rows, rows), rows)],
            dst_ref=target.at[rank, f],
            send_sem=out_sends.at[a, f, k - 1],
            recv_sem=out_recvs.at[a, f, k - 1],
            device_id=near_id(k),
            device_id_type=MESH,
        )

    def back_local(a, f):
        source, target = returns[a]
        return pltpu.make_async_copy(
            source.at[f, pl.ds(at, rows)], target.at[rank, f], out_local.at[a, f]
        )

    def sum_copy(i, f):
        return pltpu.make_async_remote_copy(
            src_ref=grad.at[f],
            dst_ref=slots.at[i, f],
            send_sem=g_sends.at[i, f],
            recv_sem=g_recvs.at[i, f],
            device_id=mate(*ring[i]),
            device_id_type=MESH,
        )

    def share(k):
        return pltpu.make_async_remote_copy(
            src_ref=grad_all.at[rank],
            dst_ref=grad_all.at[rank],
            send_sem=s_sends.at[k - 1],
            recv_sem=s_recvs.at[k - 1],
            device_id=near_id(k),
            device_id_type=MESH,
        )

    for f in range(per_rank):
        for a in range(2):
            for k in range(1, RANKS):
                near(a, f, k).start()
            local(a, f).start()

    @pl.loop(0, per_rank)
    def _(f):
        for taps, strip in ((past_taps, tp), (fore_taps, tf)):
            lines_all = jnp.broadcast_to(taps[f], (BLK, span))
            turned = pltpu.roll(lines_all, 0, 1, stride=1, stride_axis=0)
            strip[f] = turned.astype(jnp.bfloat16)

    grad[...] = jnp.zeros_like(grad)

    for f in range(per_rank):
        for a in range(2):
            local(a, f).wait()
            for k in range(1, RANKS):
                near(a, f, k).wait_recv()
            for h in range(len(halos)):
                pl.when(gives(a, h))(lambda: far(a, f, h).start())

    i0 = lax.broadcasted_iota(jnp.int32, (BLK, BLK), 0)
    i1 = lax.broadcasted_iota(jnp.int32, (BLK, BLK), 1)
    mirror = (i0 + i1 == BLK - 1).astype(jnp.bfloat16)

    @pl.loop(0, per_rank)
    def _(f):
        for a in range(2):
            for h in range(len(halos)):
                pl.when(takes(a, h))(lambda: far(a, f, h).wait_recv())
        g_ref[...] = jnp.zeros_like(g_ref)

        @pl.loop(0, own // (2 * BLK))
        def _(pair):
            starts = [pl.multiple_of(pair * 2 * BLK + i * BLK, BLK) for i in range(2)]
            place = lax.broadcasted_iota(jnp.int32, (used, cols), 0)
            xs, ys, ss = [], [], []
            for i in range(2):
                low = used - back_len[pair * 2 + i] * BLK
                high = fore_len[pair * 2 + i] * BLK
                x = past[f, pl.ds(starts[i], used)]
                xs.append(jnp.where(place >= low, x, jnp.zeros_like(x)))
                y = future[f, pl.ds(starts[i], used)]
                ys.append(jnp.where(place < high, y, jnp.zeros_like(y)))
                ss.append(y[:BLK])
            x2, y2, s2 = [jnp.concatenate(parts, 1) for parts in (xs, ys, ss)]
            ahead = jnp.dot(tp[f, :, :used], x2, preferred_element_type=jnp.float32)
            after = jnp.dot(tf[f, :, :used], y2, preferred_element_type=jnp.float32)
            flipped = jnp.dot(mirror, s2, preferred_element_type=jnp.float32)
            g_ref[:, :used] += lax.dot_general(
                flipped.astype(jnp.bfloat16),
                x2,
                (((1,), (1,)), ((), ())),
                preferred_element_type=jnp.float32,
            )
            for i in range(2):
                part = slice(i * cols, (i + 1) * cols)
                conv[f, pl.ds(starts[i], BLK)] = ahead[:, part].astype(jnp.bfloat16)
                adj[f, pl.ds(starts[i], BLK)] = after[:, part].astype(jnp.bfloat16)

        for a in range(2):
            for k in range(1, RANKS):
                back(a, f, k).start()
            back_local(a, f).start()
        aligned = pltpu.roll(g_ref[...], 0, 1, stride=1, stride_axis=0)
        sums = jnp.sum(aligned, 0, keepdims=True)
        for c in range(used // BLK):
            grad[f, c : c + 1] = sums[:, c * BLK : (c + 1) * BLK]
        for i in range(len(ring)):
            sum_copy(i, f).start()

    for i in range(len(ring)):
        for f in range(per_rank):
            sum_copy(i, f).wait_recv()
    total = grad[...]
    for i in range(len(ring)):
        total = total + slots[i]
    grad_all[rank] = total
    for k in range(1, RANKS):
        share(k).start()
    for f in range(per_rank):
        for a in range(2):
            for k in range(1, RANKS):
                near(a, f, k).wait_send()
            for h in range(len(halos)):
                pl.when(gives(a, h))(lambda: far(a, f, h).wait_send())
        for i in range(len(ring)):
            sum_copy(i, f).wait_send()
        for a in range(2):
            back_local(a, f).wait()
            for k in range(1, RANKS):
                back(a, f, k).wait()
    for k in range(1, RANKS):
        share(k).wait()


def mix(back_len, fore_len, past_taps, fore_taps, product, scaled, teams, heads, lines):
    _, per_rank, rows, cols = product.shape
    own = RANKS * rows
    span = past_taps.shape[2]
    reach = span - 2 * BLK
    others = teams * heads - 1
    halos = len(halo_parts(own, reach))
    vmem = pl.BlockSpec(memory_space=pltpu.VMEM)
    smem = pl.BlockSpec(memory_space=pltpu.SMEM)
    dma = pltpu.SemaphoreType.DMA
    out = jax.ShapeDtypeStruct((RANKS, per_rank, rows, cols), jnp.bfloat16)
    held = pltpu.VMEM((per_rank, own + reach, cols), jnp.bfloat16)
    strip = pltpu.VMEM((per_rank, BLK, span), jnp.bfloat16)
    result = pltpu.VMEM((per_rank, own, cols), jnp.bfloat16)
    grads = (per_rank, lines, BLK)
    return pl.pallas_call(
        functools.partial(mix_kernel, teams, heads, reach),
        in_specs=[smem, smem, vmem, vmem, ANY, ANY],
        out_specs=[ANY, ANY, vmem],
        out_shape=[out, out, jax.ShapeDtypeStruct((RANKS,) + grads, jnp.float32)],
        scratch_shapes=[
            held,
            held,
            strip,
            strip,
            pltpu.VMEM((BLK, span), jnp.float32),
            result,
            result,
            pltpu.VMEM(grads, jnp.float32),
            pltpu.VMEM((others,) + grads, jnp.float32),
            dma((2, per_rank, RANKS - 1)),
            dma((2, per_rank, RANKS - 1)),
            dma((2, per_rank, halos)),
            dma((2, per_rank, halos)),
            dma((2, per_rank, RANKS - 1)),
            dma((2, per_rank, RANKS - 1)),
            dma((others, per_rank)),
            dma((others, per_rank)),
            dma((RANKS - 1,)),
            dma((RANKS - 1,)),
            dma((2, per_rank)),
            dma((2, per_rank)),
        ],
        compiler_params=pltpu.CompilerParams(
            collective_id=0, has_side_effects=True, vmem_limit_bytes=56 << 20
        ),
    )(back_len, fore_len, past_taps, fore_taps, product, scaled)


def per_device(value_rows, key_rows, query_rows, cotangent, filter_taps, doc_blocks):
    rows, channels = value_rows.shape
    filters, taps_total = filter_taps.shape
    cols = channels // filters
    per_rank = filters // RANKS
    seq, heads = lax.axis_size("seq"), lax.axis_size("head")
    teams = seq // RANKS
    own = RANKS * rows
    own_blocks = own // BLK
    lags = min(MOST, taps_total // BLK)
    used = lags * BLK
    me = lax.axis_index("seq")
    rank, team = lax.rem(me, RANKS), lax.div(me, RANKS)

    product, scaled = prepare(value_rows, key_rows, query_rows, cotangent, filters)
    shape = (RANKS, per_rank, rows, cols)
    mine = lax.dynamic_slice_in_dim(filter_taps, rank * per_rank, per_rank, 0)[:, :used]
    mine = mine.astype(jnp.bfloat16).astype(jnp.float32)
    turned = mine[:, ::-1]
    gap = jnp.zeros((per_rank, BLK), jnp.float32)
    past_taps = jnp.concatenate([turned[:, BLK - 1 :], gap, turned[:, : BLK - 1]], 1)
    fore_taps = jnp.concatenate([mine, gap], 1)

    fill = jnp.full((lags - 1,), -1, jnp.int32)
    docs = jnp.concatenate([fill, doc_blocks, fill - 1], 0)
    window = lax.dynamic_slice_in_dim(docs, team * own_blocks, own_blocks + 2 * (lags - 1))
    here = window[lags - 1 : lags - 1 + own_blocks]
    back_len = sum(
        (window[lags - 1 - b : lags - 1 - b + own_blocks] == here).astype(jnp.int32)
        for b in range(lags)
    )
    fore_len = sum(
        (window[lags - 1 + b : lags - 1 + b + own_blocks] == here).astype(jnp.int32)
        for b in range(lags)
    )
    conv_all, adj_all, grad_all = mix(
        back_len, fore_len, past_taps[:, None], fore_taps[:, None],
        product.reshape(shape), scaled.reshape(shape), teams, heads, taps_total // BLK,
    )
    whole = (filters, rows, cols)
    outs = finish(
        conv_all.reshape(whole), adj_all.reshape(whole), value_rows, key_rows, query_rows, cotangent
    )
    taps_grad = grad_all.reshape(filters, taps_total)[:, :used][:, ::-1]
    taps_grad = jnp.pad(taps_grad, ((0, 0), (0, taps_total - used)))
    return (*outs, taps_grad * (1.0 / (rows * seq)))


def solution(mesh):
    rows = P("seq", "head")
    return jax.shard_map(
        per_device,
        mesh=mesh,
        in_specs=(rows, rows, rows, rows, P(), P()),
        out_specs=(rows, rows, rows, rows, P()),
        check_vma=False,
    )
```

time: 138 us -> 93.7 us (0.68)
  Pallas kernels: 114 us -> 84.4 us
  local copies, waits for them, and re-layouts: 21.1 us -> 5.22 us
    pallas_call x3 -> x1, Pallas kernels: 107 us -> 71.9 us  [mix(): pl.pallas_call(functools.partial(mix_kernel, teams, heads, reach), in_spe...]
    unnamed x41 -> x5, local copies, waits for them, and re-layouts: 19.8 us -> 2.71 us
    pallas_call x1, Pallas kernels: 4.76 us -> 8.01 us  [finish(): pl.pallas_call(functools.partial(finish_kernel, groups), grid=(steps, gro...]
    pallas_call x1, Pallas kernels: 1.71 us -> 4.53 us  [prepare(): pl.pallas_call(functools.partial(prepare_kernel, groups), grid=(steps,),...]
where the time goes in v2:
time: 93.7 us; the launch traced here: 93.2 us
  Pallas kernels  84.4 us (90%)
  local copies, waits for them, and re-layouts  5.22 us (6%)
  other arithmetic  2.83 us (3%)
    pallas_call x1, Pallas kernels, mix(): pl.pallas_call(functools.partial(mix_kernel, teams, heads, reach), in_spe...  71.9 us
    pallas_call x1, Pallas kernels, finish(): pl.pallas_call(functools.partial(finish_kernel, groups), grid=(steps, gro...  8.01 us
    pallas_call x1, Pallas kernels, prepare(): pl.pallas_call(functools.partial(prepare_kernel, groups), grid=(steps,),...  4.53 us
    unnamed x5, local copies, waits for them, and re-layouts  2.71 us

profile of v2, /device:TPU:0, one launch (start us, length us, event | category | flops | bytes accessed | tf_op | source)
XLA Modules:
  0.0 93.2 jit_solution(1201927034936764123)
XLA Ops:
  0.7 0.0 copy-start
  0.7 0.6 copy-done
  1.3 0.1 pad_add_fusion
  1.4 0.1 dynamic_slice.6
  1.5 0.7 fusion.22.fore_len
  2.1 0.6 fusion.11.back_len
  2.7 0.8 fusion
  3.5 0.1 slice.120
  3.6 0.1 slice.117
  3.7 1.0 %reverse.2 = f32[4,1536]{1,0:T(4,128)S(1)} reverse(f32[4,1536]{1,0:T(4,128)S(1)} %fusion), dimensions={1} | reverse | bytes 49152
  4.8 0.1 slice.158
  4.8 0.1 concatenate.10
  4.9 0.6 copy.11.past_taps
  5.6 0.6 broadcast_in_dim.11.fore_taps
  6.2 4.5 %shard_map.101 = (bf16[16,256,128]{2,1,0:T(8,128)(2,1)}, bf16[16,256,128]{2,1,0:T(8,128)(2,1)}) custom-call(bf16[256,2048]{1,0:T(8,128)(2,1)} %value.1, bf16[256,2048]{1,0:T(8,128)(2,1)} %value.1, bf16[256,2048]{1,0:T(8,128)(2,1)} %key.1, bf16[256,2048]{1,0:T(8,128)(2,1)} %key.1, bf16[256,2048]{1,0:T(8,128)(2,1)} %query.1, bf16[256,2048]{1,0:T(8,128)(2,1)} %query.1, ...), custom_call_target="tpu_custom_call" | custom-call | tf_op jit(solution)/shard_map/pallas_call | solution.py:48
  10.7 71.9 %shard_map.102 = (bf16[4,4,256,128]{3,2,1,0:T(8,128)(2,1)}, bf16[4,4,256,128]{3,2,1,0:T(8,128)(2,1)}, f32[4,4,16,128]{3,2,1,0:T(8,128)}) custom-call(s32[8]{0:T(128)} %fusion.11.back_len, s32[8]{0:T(128)} %fusion.22.fore_len, f32[4,1,1664]{2,1,0:T(1,128)} %copy.11.past_taps, f32[4,1,1664]{2,1,0:T(1,128)} %broadcast_in_dim.11.fore_taps, ...), custom_call_target="tpu_custom_call" | custom-call | tf_op jit(solution)/shard_map/pallas_call | solution.py:332
  82.6 0.9 %copy.14 = f32[2,8,16,128]{3,1,2,0:T(8,128)S(1)} copy(f32[2,8,16,128]{3,2,1,0:T(8,128)} %bitcast.17) | data formatting | bytes 262144
  83.6 0.9 rev.4
  84.5 0.7 pad_multiply_fusion
  85.2 8.0 %shard_map.103 = (bf16[256,2048]{1,0:T(8,128)(2,1)}, bf16[256,2048]{1,0:T(8,128)(2,1)}, bf16[256,2048]{1,0:T(8,128)(2,1)}, bf16[256,2048]{1,0:T(8,128)(2,1)}) custom-call(bf16[16,256,128]{2,1,0:T(8,128)(2,1)} %bitcast.14, bf16[16,256,128]{2,1,0:T(8,128)(2,1)} %bitcast.15, bf16[256,2048]{1,0:T(8,128)(2,1)} %value.1, bf16[256,2048]{1,0:T(8,128)(2,1)} %key.1, ...), custom_call_target="tpu_custom_call" | custom-call | tf_op jit(solution)/shard_map/pallas_call | solution.py:84
  (5 shorter events, 0.0 us)
Async XLA Ops:
  0.7 0.7 copy-start

commit v3 on v2

--- a/solution.py
+++ b/solution.py
@@ -216,21 +216,15 @@
             device_id_type=MESH,
         )
 
-    for f in range(per_rank):
+    def set_out(f):
         for a in range(2):
             for k in range(1, RANKS):
                 near(a, f, k).start()
             local(a, f).start()
 
-    @pl.loop(0, per_rank)
-    def _(f):
-        for taps, strip in ((past_taps, tp), (fore_taps, tf)):
-            lines_all = jnp.broadcast_to(taps[f], (BLK, span))
-            turned = pltpu.roll(lines_all, 0, 1, stride=1, stride_axis=0)
-            strip[f] = turned.astype(jnp.bfloat16)
-
+    for f in range(min(2, per_rank)):
+        set_out(f)
     grad[...] = jnp.zeros_like(grad)
-
     for f in range(per_rank):
         for a in range(2):
             local(a, f).wait()
@@ -238,6 +232,12 @@
                 near(a, f, k).wait_recv()
             for h in range(len(halos)):
                 pl.when(gives(a, h))(lambda: far(a, f, h).start())
+        if f + 2 < per_rank:
+            set_out(f + 2)
+        for taps, strip in ((past_taps, tp), (fore_taps, tf)):
+            lines_all = jnp.broadcast_to(taps[f], (BLK, span))
+            turned = pltpu.roll(lines_all, 0, 1, stride=1, stride_axis=0)
+            strip[f] = turned.astype(jnp.bfloat16)
 
     i0 = lax.broadcasted_iota(jnp.int32, (BLK, BLK), 0)
     i1 = lax.broadcasted_iota(jnp.int32, (BLK, BLK), 1)

time: 93.7 us -> 93.7 us (level)
  no operation moved by 1% of the time
where the time goes in v3:
time: 93.7 us; the launch traced here: 93.2 us
  Pallas kernels  84.4 us (90%)
  local copies, waits for them, and re-layouts  5.22 us (6%)
  other arithmetic  2.83 us (3%)
    pallas_call x1, Pallas kernels, mix(): pl.pallas_call(functools.partial(mix_kernel, teams, heads, reach), in_spe...  71.9 us
    pallas_call x1, Pallas kernels, finish(): pl.pallas_call(functools.partial(finish_kernel, groups), grid=(steps, gro...  8.01 us
    pallas_call x1, Pallas kernels, prepare(): pl.pallas_call(functools.partial(prepare_kernel, groups), grid=(steps,),...  4.53 us
    unnamed x5, local copies, waits for them, and re-layouts  2.71 us

profile of v3, /device:TPU:0, one launch (start us, length us, event | category | flops | bytes accessed | tf_op | source)
XLA Modules:
  0.0 93.2 jit_solution(14158309710889325743)
XLA Ops:
  0.7 0.0 copy-start
  0.7 0.6 copy-done
  1.3 0.1 pad_add_fusion
  1.4 0.1 dynamic_slice.6
  1.5 0.7 fusion.22.fore_len
  2.1 0.6 fusion.11.back_len
  2.7 0.8 fusion
  3.5 0.1 slice.120
  3.6 0.1 slice.117
  3.7 1.0 %reverse.2 = f32[4,1536]{1,0:T(4,128)S(1)} reverse(f32[4,1536]{1,0:T(4,128)S(1)} %fusion), dimensions={1} | reverse | bytes 49152
  4.8 0.1 slice.158
  4.8 0.1 concatenate.10
  4.9 0.6 copy.11.past_taps
  5.6 0.6 broadcast_in_dim.11.fore_taps
  6.2 4.5 %shard_map.101 = (bf16[16,256,128]{2,1,0:T(8,128)(2,1)}, bf16[16,256,128]{2,1,0:T(8,128)(2,1)}) custom-call(bf16[256,2048]{1,0:T(8,128)(2,1)} %value.1, bf16[256,2048]{1,0:T(8,128)(2,1)} %value.1, bf16[256,2048]{1,0:T(8,128)(2,1)} %key.1, bf16[256,2048]{1,0:T(8,128)(2,1)} %key.1, bf16[256,2048]{1,0:T(8,128)(2,1)} %query.1, bf16[256,2048]{1,0:T(8,128)(2,1)} %query.1, ...), custom_call_target="tpu_custom_call" | custom-call | tf_op jit(solution)/shard_map/pallas_call | solution.py:48
  10.7 71.9 %shard_map.102 = (bf16[4,4,256,128]{3,2,1,0:T(8,128)(2,1)}, bf16[4,4,256,128]{3,2,1,0:T(8,128)(2,1)}, f32[4,4,16,128]{3,2,1,0:T(8,128)}) custom-call(s32[8]{0:T(128)} %fusion.11.back_len, s32[8]{0:T(128)} %fusion.22.fore_len, f32[4,1,1664]{2,1,0:T(1,128)} %copy.11.past_taps, f32[4,1,1664]{2,1,0:T(1,128)} %broadcast_in_dim.11.fore_taps, ...), custom_call_target="tpu_custom_call" | custom-call | tf_op jit(solution)/shard_map/pallas_call | solution.py:332
  82.6 0.9 %copy.14 = f32[2,8,16,128]{3,1,2,0:T(8,128)S(1)} copy(f32[2,8,16,128]{3,2,1,0:T(8,128)} %bitcast.17) | data formatting | bytes 262144
  83.6 0.9 rev.4
  84.5 0.7 pad_multiply_fusion
  85.2 8.0 %shard_map.103 = (bf16[256,2048]{1,0:T(8,128)(2,1)}, bf16[256,2048]{1,0:T(8,128)(2,1)}, bf16[256,2048]{1,0:T(8,128)(2,1)}, bf16[256,2048]{1,0:T(8,128)(2,1)}) custom-call(bf16[16,256,128]{2,1,0:T(8,128)(2,1)} %bitcast.14, bf16[16,256,128]{2,1,0:T(8,128)(2,1)} %bitcast.15, bf16[256,2048]{1,0:T(8,128)(2,1)} %value.1, bf16[256,2048]{1,0:T(8,128)(2,1)} %key.1, ...), custom_call_target="tpu_custom_call" | custom-call | tf_op jit(solution)/shard_map/pallas_call | solution.py:84
  (5 shorter events, 0.0 us)
Async XLA Ops:
  0.7 0.7 copy-start
